TPU v7x, 32 devices: a whole 2x2x4 slice. The times are simulated.
32 devices in a mesh: order: 4 (over y, core), basin: 8 (over z, x).
Axes of the slice: x: 2, y: 2, z: 4, core: 2. Of those that a mesh axis runs over, the one named last changes fastest.
Arguments:
- forcings: bfloat16 [32, 16, 16384], P(None, None, ('order', 'basin')), may hold values from -6 to 6
- w_input: bfloat16 [512, 16], replicated, may hold values from -1.5 to 1.5
- w_recur: bfloat16 [512, 128], replicated, may hold values from -0.5 to 0.5
- gate_bias: float32 [512], replicated, may hold values from -3 to 3
- w_runoff: float32 [128], replicated, may hold values from -0.5 to 0.5
- travel_time: float32 [16384], P(('order', 'basin')), may hold values from 1 to 8
- weight_x: float32 [16384], P(('order', 'basin')), may hold values from 0 to 0.3
- drain_basin: int32 [16384, 1], P(('order', 'basin')), may hold values from 0 to 7; in each aligned block of 512 rows (0 to 511, 512 to 1023, ...) at most 128 rows name the same one
- drain_reach: int32 [16384, 1], P(('order', 'basin')), may hold values from 0 to 511
Outputs:
- discharge: float32 [32, 16384], P(None, ('order', 'basin'))
Inputs may be any that keep to these rules, and one draw needn't show every extreme that they name: `drain_basin`: among the reaches of one device (aligned blocks of 512 reaches), at most 128 drain to the same basin index, and exactly 128 do for some basin index in some block.
All inputs are finite; a program needn't handle non-finite values.
Results may differ from a plain program's by a relative error of at most 0.0003.
Values sent between devices are 32-bit elements; how exact they have to be, the bound alone decides.
No kernel may reach another device: no remote copies, remote signals or barrier semaphores. Data moves between devices by JAX's collectives and lax.ppermute only.
A program may use at most 64 MiB of HBM per device.

v0:
```python
import functools

import jax
import jax.numpy as jnp
from jax import lax
from jax.experimental import pallas as pl
from jax.experimental.pallas import tpu as pltpu
from jax.sharding import PartitionSpec as P

F32 = jnp.float32
BF16 = jnp.bfloat16
ID_ROWS = 8
CHUNK = 256


def vmem():
    return pl.BlockSpec(memory_space=pltpu.VMEM)


def call(body, out_shape, megabytes=8, **more):
    return pl.pallas_call(
        body,
        out_shape=out_shape,
        out_specs=jax.tree.map(lambda _: vmem(), out_shape),
        compiler_params=pltpu.CompilerParams(vmem_limit_bytes=megabytes << 20),
        **more,
    )


def delayed(series, days):
    return jnp.concatenate(
        [jnp.zeros((days, series.shape[1]), series.dtype), series[: series.shape[0] - days]], axis=0
    )


def routing_coefficients(travel_time, weight_x):
    held = travel_time * (1.0 - weight_x)
    denominator = held + 0.5
    coeff_first = (0.5 - travel_time * weight_x) / denominator
    coeff_second = (0.5 + travel_time * weight_x) / denominator
    recession = (held - 0.5) / denominator
    return coeff_first, coeff_first * recession + coeff_second, recession


def route(inflow, coefficients):
    first, later, recession = coefficients
    stored, power, reach = inflow, recession, 1
    while reach < inflow.shape[0]:
        stored = stored + power * delayed(stored, reach)
        power, reach = power * power, 2 * reach
    return first * inflow + later * delayed(stored, 1)


def in_halves(values):
    high = values.astype(BF16)
    return jnp.concatenate([high, (values - high.astype(F32)).astype(BF16)], axis=0)


def choose(values, table):
    both = jnp.dot(in_halves(values), table, preferred_element_type=F32)
    return both[: values.shape[0]] + both[values.shape[0] :]


def as_column(row):
    return jnp.transpose(jnp.broadcast_to(row, (8, row.shape[1])))[:, :1]


def one_hot(index_column, width):
    lanes = lax.broadcasted_iota(jnp.int32, (index_column.shape[0], width), 1).astype(F32)
    return jnp.where(index_column == lanes, 1.0, 0.0).astype(BF16)


def lay_out(ref, rows, first_row=0):
    count = rows.shape[0]
    if len(ref.shape) == 2:
        ref[first_row : first_row + count, :] = rows
    else:
        capacity = ref.shape[2]
        for basin in range(ref.shape[0]):
            ref[basin, first_row : first_row + count, :] = rows[
                :, basin * capacity : (basin + 1) * capacity
            ]


def take_in(ref, first_row, count):
    if len(ref.shape) == 2:
        return ref[first_row : first_row + count, :]
    return jnp.concatenate(
        [ref[basin, first_row : first_row + count, :] for basin in range(ref.shape[0])], axis=1
    )


def send_slots(drain_to, basins, capacity):
    reaches = drain_to.shape[1]
    basin_rows = max(basins, 8)
    member = (lax.broadcasted_iota(jnp.int32, (basin_rows, reaches), 0) == drain_to).astype(F32)
    before = lax.broadcasted_iota(jnp.int32, (reaches, reaches), 0)
    after = lax.broadcasted_iota(jnp.int32, (reaches, reaches), 1)
    upper = jnp.where(before < after, 1.0, 0.0).astype(BF16)
    earlier = jnp.dot(member.astype(BF16), upper, preferred_element_type=F32)
    rank = jnp.sum(member * earlier, axis=0, keepdims=True)
    return drain_to.astype(F32) * capacity + rank


def first_body(
    forcings_ref,
    w_input_ref,
    w_recur_ref,
    gate_bias_ref,
    w_runoff_ref,
    params_ref,
    drain_ref,
    runoff_ref,
    coefficients_ref,
    send_table_ref,
    outgoing_ref,
    weights,
    sums,
    *,
    days,
    basins,
):
    reaches = forcings_ref.shape[1]
    channels = forcings_ref.shape[0] // days
    units = w_recur_ref.shape[1]
    gates = 4 * units
    per_block = units // channels
    capacity = 2 * reaches // basins

    gate_lane = lax.broadcasted_iota(jnp.int32, (1, gates), 1)
    is_candidate = (gate_lane >= 2 * units) & (gate_lane < 3 * units)
    scale = jnp.where(is_candidate, 1.0, 0.5)
    recur = (jnp.transpose(w_recur_ref[...].astype(F32)) * (0.5 * scale)).astype(BF16)
    inputs = (jnp.transpose(w_input_ref[...].astype(F32)) * scale).astype(BF16)
    bias = gate_bias_ref[...] * scale
    readout = 0.5 * w_runoff_ref[...]
    for day in range(per_block):
        weights[day, :units, :] = recur
        weights[day, units:, :] = jnp.zeros((units, gates), BF16)
        weights[day, units + day * channels : units + (day + 1) * channels, :] = inputs
    sums[...] = jnp.zeros_like(sums)
    chunk = min(CHUNK, reaches)
    chunks = reaches // chunk
    lane = lax.broadcasted_iota(jnp.int32, (chunk, units), 1)

    def block_of_days(block, state):
        rows = pl.ds(pl.multiple_of(block * units, units), units)
        forced = jnp.transpose(forcings_ref[rows, :].astype(F32)).astype(BF16)
        state = list(state)
        for day in range(per_block):
            for part in range(chunks):
                hidden, memory = state[part]
                span = slice(part * chunk, (part + 1) * chunk)
                gate_sums = bias + jnp.dot(
                    jnp.concatenate([hidden, forced[span]], axis=1),
                    weights[day],
                    preferred_element_type=F32,
                )
                ingate = jnp.tanh(gate_sums[:, :units])
                forget = jnp.tanh(gate_sums[:, units : 2 * units])
                candidate = jnp.tanh(gate_sums[:, 2 * units : 3 * units])
                outgate = jnp.tanh(gate_sums[:, 3 * units :])
                memory = 0.5 * ((forget * memory + memory) + (ingate * candidate + candidate))
                squashed = jnp.tanh(memory)
                hidden = (outgate * squashed + squashed).astype(BF16)
                drained = jnp.sum(hidden.astype(F32) * readout, axis=1, keepdims=True)
                sums[span, :] = jnp.where(lane == block * per_block + day, drained, sums[span, :])
                state[part] = (hidden, memory)
        return tuple(state)

    state = tuple(
        (jnp.zeros((chunk, units), BF16), jnp.zeros((chunk, units), F32)) for _ in range(chunks)
    )
    lax.fori_loop(0, days // per_block, block_of_days, state)
    pre = jnp.transpose(sums[...])[:days]
    runoff = jnp.maximum(pre, 0.0) + jnp.log1p(jnp.exp(-jnp.abs(pre)))
    runoff_ref[...] = runoff

    coefficients = routing_coefficients(params_ref[0:1, :], params_ref[1:2, :])
    for row in range(3):
        coefficients_ref[row : row + 1, :] = coefficients[row]
    slots = send_slots(drain_ref[0:1, :], basins, capacity)
    send_table = one_hot(as_column(slots), basins * capacity)
    send_table_ref[...] = send_table
    reach = drain_ref[1:2, :]
    digits = jnp.concatenate([reach // 16, reach % 16, jnp.zeros((6, reaches), jnp.int32)], axis=0)
    found = jnp.dot(digits.astype(F32).astype(BF16), send_table, preferred_element_type=F32)
    targets = 16.0 * found[0:1] + found[1:2]
    lay_out(outgoing_ref, choose(route(runoff, coefficients), send_table))
    lay_out(outgoing_ref, jnp.broadcast_to(targets, (ID_ROWS, basins * capacity)), days)


def first_unpack_body(received_ref, arrive_ref, recv_table_ref):
    days, reaches = arrive_ref.shape
    targets = take_in(received_ref, days, 1)
    recv_table = one_hot(as_column(targets), reaches)
    recv_table_ref[...] = recv_table
    arrive_ref[...] = choose(take_in(received_ref, 0, days), recv_table)


def unpack_body(received_ref, recv_table_ref, arrive_ref):
    arrive_ref[...] = choose(take_in(received_ref, 0, arrive_ref.shape[0]), recv_table_ref[...])


def coefficient_rows(ref):
    return tuple(ref[row : row + 1, :] for row in range(3))


def pack_body(*refs):
    runoff_ref, coefficients_ref, send_table_ref, *arrive_refs, outgoing_ref = refs
    inflow = runoff_ref[...]
    for ref in arrive_refs:
        inflow = inflow + ref[...]
    routed = route(inflow, coefficient_rows(coefficients_ref))
    lay_out(outgoing_ref, choose(routed, send_table_ref[...]))


def last_body(*refs):
    runoff_ref, coefficients_ref, *arrive_refs, out_ref = refs
    inflow = runoff_ref[...]
    for ref in arrive_refs:
        inflow = inflow + ref[...]
    out_ref[...] = route(inflow, coefficient_rows(coefficients_ref))


def per_device(
    forcings, w_input, w_recur, gate_bias, w_runoff, travel_time, weight_x, drain_basin, drain_reach
):
    basins = lax.axis_size("basin")
    groups = lax.axis_size("order")
    days, channels, reaches = forcings.shape
    units = w_recur.shape[1]
    capacity = 2 * reaches // basins
    slots = basins * capacity
    split = capacity % 128 == 0

    def payload(rows):
        return jax.ShapeDtypeStruct((basins, rows, capacity) if split else (rows, slots), F32)

    def series():
        return jax.ShapeDtypeStruct((days, reaches), F32)

    def exchange(outgoing):
        if split:
            return lax.all_to_all(outgoing, "basin", split_axis=0, concat_axis=0, tiled=True)
        outgoing = outgoing.reshape(-1, basins, capacity)
        received = lax.all_to_all(outgoing, "basin", split_axis=1, concat_axis=1, tiled=True)
        return received.reshape(-1, slots)

    params = jnp.stack([travel_time, weight_x])
    drain = jnp.stack([drain_basin[:, 0], drain_reach[:, 0]])
    runoff, coefficients, send_table, outgoing = call(
        functools.partial(first_body, days=days, basins=basins),
        [
            series(),
            jax.ShapeDtypeStruct((3, reaches), F32),
            jax.ShapeDtypeStruct((reaches, slots), BF16),
            payload(days + ID_ROWS),
        ],
        megabytes=24,
        scratch_shapes=[
            pltpu.VMEM((units // channels, 2 * units, 4 * units), BF16),
            pltpu.VMEM((reaches, units), F32),
        ],
    )(
        forcings.reshape(days * channels, reaches),
        w_input,
        w_recur,
        gate_bias[None, :],
        w_runoff[None, :],
        params,
        drain,
    )
    arrivals = []
    recv_table = None
    for section in range(groups - 1):
        if section > 0:
            outgoing = call(pack_body, payload(days))(runoff, coefficients, send_table, *arrivals)
        received = exchange(outgoing)
        if section == 0:
            arrive, recv_table = call(
                first_unpack_body, [series(), jax.ShapeDtypeStruct((slots, reaches), BF16)]
            )(received)
        else:
            arrive = call(unpack_body, series())(received, recv_table)
        pairs = [
            (section * basins + basin, (section + 1) * basins + basin) for basin in range(basins)
        ]
        arrivals.append(lax.ppermute(arrive, ("order", "basin"), pairs))
    return call(last_body, series())(runoff, coefficients, *arrivals)


def solution(mesh):
    return jax.shard_map(
        per_device,
        mesh=mesh,
        in_specs=(
            P(None, None, ("order", "basin")),
            P(),
            P(),
            P(),
            P(),
            P(("order", "basin")),
            P(("order", "basin")),
            P(("order", "basin"), None),
            P(("order", "basin"), None),
        ),
        out_specs=P(None, ("order", "basin")),
        check_vma=False,
    )
```

profile of v0, /device:TPU:5, one launch (start us, length us, event | category | flops | bytes accessed | tf_op | source)
XLA Modules:
  0.0 57.3 jit_solution(16287523623412873040)
XLA Ops:
  0.0 0.0 copy-start.1
  0.0 0.0 copy-start.5
  0.0 0.9 %copy.10.w_input_ref = bf16[512,16]{1,0:T(8,128)(2,1)S(1)} copy(bf16[512,16]{0,1:T(8,128)(2,1)} %param.10) | data formatting | bytes 32768 | tf_op args[1]
  0.9 0.0 copy-start.4
  0.9 0.0 copy-done.5
  0.9 0.7 %copy-done.4 = f32[512]{0:T(512)S(1)} copy-done((f32[512]{0:T(512)S(1)}, f32[512]{0:T(512)}, u32[]{:S(2)}) %copy-start.4) | copy-done | bytes 2072
  1.6 0.0 copy-start.7
  1.6 0.0 copy-start.6
  1.6 0.7 %copy-done.7 = s32[512,1]{0,1:T(1,128)S(1)} copy-done((s32[512,1]{0,1:T(1,128)S(1)}, s32[512,1]{0,1:T(1,128)}, u32[]{:S(2)}) %copy-start.7) | copy-done | bytes 2072
  2.3 0.0 copy-done.6
  2.3 0.0 copy-start.2
  2.3 0.0 copy-start.3
  2.3 0.0 copy-done.1
  2.3 0.7 %copy-done.2 = f32[512]{0:T(512)S(1)} copy-done((f32[512]{0:T(512)S(1)}, f32[512]{0:T(512)}, u32[]{:S(2)}) %copy-start.2) | copy-done | bytes 2072
  3.0 0.0 copy-done.3
  3.0 0.0 copy-start
  3.0 1.0 %copy-done = bf16[32,16,512]{2,1,0:T(8,128)(2,1)S(1)} copy-done((bf16[32,16,512]{2,1,0:T(8,128)(2,1)S(1)}, bf16[32,16,512]{2,1,0:T(8,128)(2,1)}, u32[]{:S(2)}) %copy-start) | copy-done | bytes 524312
  4.0 9.0 %shard_map.91 = (f32[32,512]{1,0:T(8,128)S(1)}, f32[3,512]{1,0:T(4,128)S(1)}, bf16[512,1024]{1,0:T(8,128)(2,1)S(1)}, f32[8,40,128]{2,1,0:T(8,128)S(1)}) custom-call(bf16[512,512]{1,0:T(8,128)(2,1)S(1)} %bitcast.7, bf16[512,16]{1,0:T(8,128)(2,1)S(1)} %copy.10.w_input_ref, bf16[512,128]{1,0:T(8,128)(2,1)S(1)} %copy-done.1, f32[1,512]{1,0:T(1,128)S(1)} %bitcast.8, ...), custom_call_target="tpu_custom_call" | custom-call | tf_op jit(solution)/shard_map/pallas_call | solution.py:252
  13.0 11.7 %all_to_all.15.received_ref = f32[8,40,128]{2,1,0:T(8,128)S(1)} all-to-all(f32[8,40,128]{2,1,0:T(8,128)S(1)} %get-tuple-element.13), channel_id=1, replica_groups=mesh['order'=4,'basin'=8] {'basin'}, dimensions={0} | all-to-all | bytes 327680 | tf_op jit(solution)/shard_map/all_to_all | solution.py:245
  24.7 0.6 %shard_map.92 = (f32[32,512]{1,0:T(8,128)S(1)}, bf16[1024,512]{1,0:T(8,128)(2,1)S(1)}) custom-call(f32[8,40,128]{2,1,0:T(8,128)S(1)} %all_to_all.15.received_ref), custom_call_target="tpu_custom_call" | custom-call | tf_op jit(solution)/shard_map/pallas_call | solution.py:281
  25.3 0.7 %collective-permute-start = (f32[32,512]{1,0:T(8,128)S(1)}, f32[32,512]{1,0:T(8,128)S(1)}, u32[]{:S(2)}, u32[]{:S(2)}) collective-permute-start(f32[32,512]{1,0:T(8,128)S(1)} %get-tuple-element.14), channel_id=1, source_target_pairs={{0,8},{1,9},{2,10},{3,11},{4,12},{5,13},{6,14},{7,15}} | collective-permute-start | bytes 196616 | tf_op jit(solution)/shard_map/ppermute | solution.py:289
  26.0 0.0 collective-permute-done.refs_3_.refs_2_
  26.0 0.3 shard_map.93
  26.3 9.6 %all_to_all.16.received_ref = f32[8,32,128]{2,1,0:T(8,128)S(1)} all-to-all(f32[8,32,128]{2,1,0:T(8,128)S(1)} %shard_map.93), channel_id=1, replica_groups=mesh['order'=4,'basin'=8] {'basin'}, dimensions={0} | all-to-all | bytes 262144 | tf_op jit(solution)/shard_map/all_to_all | solution.py:245
  35.9 0.3 shard_map.94
  36.2 0.7 %collective-permute-start.1 = (f32[32,512]{1,0:T(8,128)S(1)}, f32[32,512]{1,0:T(8,128)S(1)}, u32[]{:S(2)}, u32[]{:S(2)}) collective-permute-start(f32[32,512]{1,0:T(8,128)S(1)} %shard_map.94), channel_id=1, source_target_pairs={{8,16},{9,17},{10,18},{11,19},{12,20},{13,21},{14,22},{15,23}} | collective-permute-start | bytes 196616 | tf_op jit(solution)/shard_map/ppermute | solution.py:289
  36.8 0.0 collective-permute-done.1.refs_4_.refs_3_
  36.9 0.3 shard_map.95
  37.2 8.6 %all_to_all.17.received_ref = f32[8,32,128]{2,1,0:T(8,128)S(1)} all-to-all(f32[8,32,128]{2,1,0:T(8,128)S(1)} %shard_map.95), channel_id=1, replica_groups=mesh['order'=4,'basin'=8] {'basin'}, dimensions={0} | all-to-all | bytes 262144 | tf_op jit(solution)/shard_map/all_to_all | solution.py:245
  45.8 0.3 shard_map.96
  46.0 1.3 %collective-permute-start.2 = (f32[32,512]{1,0:T(8,128)S(1)}, f32[32,512]{1,0:T(8,128)S(1)}, u32[]{:S(2)}, u32[]{:S(2)}) collective-permute-start(f32[32,512]{1,0:T(8,128)S(1)} %shard_map.96), channel_id=1, source_target_pairs={{16,24},{17,25},{18,26},{19,27},{20,28},{21,29},{22,30},{23,31}} | collective-permute-start | bytes 196616 | tf_op jit(solution)/shard_map/ppermute | solution.py:289
  47.3 9.2 %collective-permute-done.2.refs_4_ = f32[32,512]{1,0:T(8,128)S(1)} collective-permute-done((f32[32,512]{1,0:T(8,128)S(1)}, f32[32,512]{1,0:T(8,128)S(1)}, u32[]{:S(2)}, u32[]{:S(2)}) %collective-permute-start.2) | collective-permute-done | bytes 65568 | tf_op jit(solution)/shard_map/ppermute | solution.py:289
  56.6 0.7 %shard_map.97 = f32[32,512]{1,0:T(8,128)} custom-call(f32[32,512]{1,0:T(8,128)S(1)} %get-tuple-element.11.refs_0_, f32[3,512]{1,0:T(4,128)S(1)} %get-tuple-element.12.refs_1_, f32[32,512]{1,0:T(8,128)S(1)} %collective-permute-done.refs_3_.refs_2_, f32[32,512]{1,0:T(8,128)S(1)} %collective-permute-done.1.refs_4_.refs_3_, ...), custom_call_target="tpu_custom_call" | custom-call | tf_op jit(solution)/shard_map/pallas_call | solution.py:290
  (2 shorter events, 0.0 us)
Async XLA Ops:
  0.0 2.3 %copy-start.1 = (bf16[512,128]{1,0:T(8,128)(2,1)S(1)}, bf16[512,128]{1,0:T(8,128)(2,1)}, u32[]{:S(2)}) copy-start(bf16[512,128]{1,0:T(8,128)(2,1)} %w_recur_ref.1) | copy-start | bytes 393220
  0.0 0.9 %copy-start.5 = (f32[512]{0:T(512)S(1)}, f32[512]{0:T(512)}, u32[]{:S(2)}) copy-start(f32[512]{0:T(512)} %param.14) | copy-start | bytes 6148
  0.9 0.7 %copy-start.4 = (f32[512]{0:T(512)S(1)}, f32[512]{0:T(512)}, u32[]{:S(2)}) copy-start(f32[512]{0:T(512)} %param.15) | copy-start | bytes 6148
  1.6 0.7 %copy-start.7 = (s32[512,1]{0,1:T(1,128)S(1)}, s32[512,1]{0,1:T(1,128)}, u32[]{:S(2)}) copy-start(s32[512,1]{0,1:T(1,128)} %param.16) | copy-start | bytes 6148
  1.6 0.7 %copy-start.6 = (s32[512,1]{0,1:T(1,128)S(1)}, s32[512,1]{0,1:T(1,128)}, u32[]{:S(2)}) copy-start(s32[512,1]{0,1:T(1,128)} %param.17) | copy-start | bytes 6148
  2.3 0.7 %copy-start.2 = (f32[512]{0:T(512)S(1)}, f32[512]{0:T(512)}, u32[]{:S(2)}) copy-start(f32[512]{0:T(512)} %param.12) | copy-start | bytes 6148
  2.3 0.7 %copy-start.3 = (f32[128]{0:T(128)S(1)}, f32[128]{0:T(128)}, u32[]{:S(2)}) copy-start(f32[128]{0:T(128)} %param.13) | copy-start | bytes 1540
  3.0 1.0 %copy-start = (bf16[32,16,512]{2,1,0:T(8,128)(2,1)S(1)}, bf16[32,16,512]{2,1,0:T(8,128)(2,1)}, u32[]{:S(2)}) copy-start(bf16[32,16,512]{2,1,0:T(8,128)(2,1)} %param.9) | copy-start | bytes 1572868
  25.3 0.7 %collective-permute-start = (f32[32,512]{1,0:T(8,128)S(1)}, f32[32,512]{1,0:T(8,128)S(1)}, u32[]{:S(2)}, u32[]{:S(2)}) collective-permute-start(f32[32,512]{1,0:T(8,128)S(1)} %get-tuple-element.14), channel_id=1, source_target_pairs={{0,8},{1,9},{2,10},{3,11},{4,12},{5,13},{6,14},{7,15}} | collective-permute-start | bytes 196616 | tf_op jit(solution)/shard_map/ppermute | solution.py:289
  36.2 0.7 %collective-permute-start.1 = (f32[32,512]{1,0:T(8,128)S(1)}, f32[32,512]{1,0:T(8,128)S(1)}, u32[]{:S(2)}, u32[]{:S(2)}) collective-permute-start(f32[32,512]{1,0:T(8,128)S(1)} %shard_map.94), channel_id=1, source_target_pairs={{8,16},{9,17},{10,18},{11,19},{12,20},{13,21},{14,22},{15,23}} | collective-permute-start | bytes 196616 | tf_op jit(solution)/shard_map/ppermute | solution.py:289
  46.0 10.5 %collective-permute-start.2 = (f32[32,512]{1,0:T(8,128)S(1)}, f32[32,512]{1,0:T(8,128)S(1)}, u32[]{:S(2)}, u32[]{:S(2)}) collective-permute-start(f32[32,512]{1,0:T(8,128)S(1)} %shard_map.96), channel_id=1, source_target_pairs={{16,24},{17,25},{18,26},{19,27},{20,28},{21,29},{22,30},{23,31}} | collective-permute-start | bytes 196616 | tf_op jit(solution)/shard_map/ppermute | solution.py:289
where the time goes:
time: 57.7 us; the launch traced here: 57.3 us
  blocking collectives  29.9 us (52%)
  Pallas kernels  11.4 us (20%)
  waiting for transfers between devices  9.23 us (16%)
  local copies, waits for them, and re-layouts  3.95 us (7%)
  starting transfers between devices  2.66 us (5%)
    all_to_all x3, blocking collectives, exchange(): lax.all_to_all(outgoing, 'basin', split_axis=0, concat_axis=0, tiled=True)  29.9 us
    ppermute x3, waiting for transfers between devices, per_device(): arrivals.append(lax.ppermute(arrive, ('order', 'basin'), pairs))  9.23 us
    pallas_call x1, Pallas kernels, per_device(): call(functools.partial(first_body, days=days, basins=basins), [series(),...  8.96 us
    unnamed x17, local copies, waits for them, and re-layouts  3.95 us
    ppermute x3, starting transfers between devices, per_device(): arrivals.append(lax.ppermute(arrive, ('order', 'basin'), pairs))  2.66 us
  transfers between devices with their start and end apart: 3, of which 1 were waited for; matrix products, arithmetic and copies ran while one was open for 0% of the time, Pallas kernels for 0%

commit v1 on v0

--- a/solution.py
+++ b/solution.py
@@ -103,45 +103,90 @@
 
 
 def first_body(
+    forcings_hbm,
+    w_input_hbm,
+    w_recur_hbm,
+    gate_bias_hbm,
+    w_runoff_hbm,
+    travel_hbm,
+    weight_hbm,
+    drain_basin_hbm,
+    drain_reach_hbm,
+    runoff_ref,
+    coefficients_ref,
+    send_table_ref,
+    targets_ref,
     forcings_ref,
     w_input_ref,
     w_recur_ref,
     gate_bias_ref,
     w_runoff_ref,
-    params_ref,
-    drain_ref,
-    runoff_ref,
-    coefficients_ref,
-    send_table_ref,
-    outgoing_ref,
+    travel_ref,
+    weight_ref,
+    drain_basin_ref,
+    drain_reach_ref,
     weights,
     sums,
+    arrived,
     *,
     days,
     basins,
 ):
+    loads = [
+        pltpu.make_async_copy(source, target, arrived.at[number])
+        for number, (source, target) in enumerate(
+            [
+                (w_recur_hbm, w_recur_ref),
+                (w_input_hbm, w_input_ref),
+                (gate_bias_hbm, gate_bias_ref),
+                (w_runoff_hbm, w_runoff_ref),
+                (travel_hbm, travel_ref),
+                (weight_hbm, weight_ref),
+                (drain_basin_hbm, drain_basin_ref),
+                (drain_reach_hbm, drain_reach_ref),
+                (forcings_hbm, forcings_ref),
+            ]
+        )
+    ]
+    for load in loads:
+        load.start()
     reaches = forcings_ref.shape[1]
     channels = forcings_ref.shape[0] // days
     units = w_recur_ref.shape[1]
     gates = 4 * units
     per_block = units // channels
     capacity = 2 * reaches // basins
+    sums[...] = jnp.zeros_like(sums)
+    for day in range(per_block):
+        weights[day, units:, :] = jnp.zeros((units, gates), BF16)
+    for load in loads[:-1]:
+        load.wait()
 
     gate_lane = lax.broadcasted_iota(jnp.int32, (1, gates), 1)
     is_candidate = (gate_lane >= 2 * units) & (gate_lane < 3 * units)
     scale = jnp.where(is_candidate, 1.0, 0.5)
     recur = (jnp.transpose(w_recur_ref[...].astype(F32)) * (0.5 * scale)).astype(BF16)
-    inputs = (jnp.transpose(w_input_ref[...].astype(F32)) * scale).astype(BF16)
+    inputs = (w_input_ref[...].astype(F32) * scale).astype(BF16)
     bias = gate_bias_ref[...] * scale
     readout = 0.5 * w_runoff_ref[...]
     for day in range(per_block):
         weights[day, :units, :] = recur
-        weights[day, units:, :] = jnp.zeros((units, gates), BF16)
         weights[day, units + day * channels : units + (day + 1) * channels, :] = inputs
-    sums[...] = jnp.zeros_like(sums)
     chunk = min(CHUNK, reaches)
     chunks = reaches // chunk
     lane = lax.broadcasted_iota(jnp.int32, (chunk, units), 1)
+
+    coefficients = routing_coefficients(travel_ref[...], weight_ref[...])
+    for row in range(3):
+        coefficients_ref[row : row + 1, :] = coefficients[row]
+    slots = send_slots(drain_basin_ref[...], basins, capacity)
+    send_table = one_hot(as_column(slots), basins * capacity)
+    send_table_ref[...] = send_table
+    reach = drain_reach_ref[...]
+    digits = jnp.concatenate([reach // 16, reach % 16, jnp.zeros((6, reaches), jnp.int32)], axis=0)
+    found = jnp.dot(digits.astype(F32).astype(BF16), send_table, preferred_element_type=F32)
+    targets_ref[...] = jnp.broadcast_to(16.0 * found[0:1] + found[1:2], targets_ref.shape)
+    loads[-1].wait()
 
     def block_of_days(block, state):
         rows = pl.ds(pl.multiple_of(block * units, units), units)
@@ -176,51 +221,38 @@
     runoff = jnp.maximum(pre, 0.0) + jnp.log1p(jnp.exp(-jnp.abs(pre)))
     runoff_ref[...] = runoff
 
-    coefficients = routing_coefficients(params_ref[0:1, :], params_ref[1:2, :])
-    for row in range(3):
-        coefficients_ref[row : row + 1, :] = coefficients[row]
-    slots = send_slots(drain_ref[0:1, :], basins, capacity)
-    send_table = one_hot(as_column(slots), basins * capacity)
-    send_table_ref[...] = send_table
-    reach = drain_ref[1:2, :]
-    digits = jnp.concatenate([reach // 16, reach % 16, jnp.zeros((6, reaches), jnp.int32)], axis=0)
-    found = jnp.dot(digits.astype(F32).astype(BF16), send_table, preferred_element_type=F32)
-    targets = 16.0 * found[0:1] + found[1:2]
-    lay_out(outgoing_ref, choose(route(runoff, coefficients), send_table))
-    lay_out(outgoing_ref, jnp.broadcast_to(targets, (ID_ROWS, basins * capacity)), days)
-
-
-def first_unpack_body(received_ref, arrive_ref, recv_table_ref):
+
+def pack_body(runoff_ref, coefficients_ref, send_table_ref, targets_ref, arrive_ref, outgoing_ref):
+    routed = route(runoff_ref[...] + arrive_ref[...], coefficient_rows(coefficients_ref))
+    lay_out(outgoing_ref, choose(routed, send_table_ref[...]))
+    lay_out(outgoing_ref, targets_ref[...], routed.shape[0])
+
+
+def unpack_body(received_ref, arrive_ref):
     days, reaches = arrive_ref.shape
-    targets = take_in(received_ref, days, 1)
-    recv_table = one_hot(as_column(targets), reaches)
-    recv_table_ref[...] = recv_table
+    recv_table = one_hot(as_column(take_in(received_ref, days, 1)), reaches)
     arrive_ref[...] = choose(take_in(received_ref, 0, days), recv_table)
 
 
-def unpack_body(received_ref, recv_table_ref, arrive_ref):
-    arrive_ref[...] = choose(take_in(received_ref, 0, arrive_ref.shape[0]), recv_table_ref[...])
+def last_body(runoff_ref, coefficients_ref, arrive_ref, out_ref):
+    out_ref[...] = route(
+        runoff_ref[...] + arrive_ref[...], coefficient_rows(coefficients_ref)
+    )
 
 
 def coefficient_rows(ref):
     return tuple(ref[row : row + 1, :] for row in range(3))
 
 
-def pack_body(*refs):
-    runoff_ref, coefficients_ref, send_table_ref, *arrive_refs, outgoing_ref = refs
-    inflow = runoff_ref[...]
-    for ref in arrive_refs:
-        inflow = inflow + ref[...]
-    routed = route(inflow, coefficient_rows(coefficients_ref))
-    lay_out(outgoing_ref, choose(routed, send_table_ref[...]))
-
-
-def last_body(*refs):
-    runoff_ref, coefficients_ref, *arrive_refs, out_ref = refs
-    inflow = runoff_ref[...]
-    for ref in arrive_refs:
-        inflow = inflow + ref[...]
-    out_ref[...] = route(inflow, coefficient_rows(coefficients_ref))
+def handed_on(passed, section, groups, basins):
+    turned = [(2 * section + 1 - group) % groups for group in range(groups)]
+    pairs = [
+        (group * basins + basin, turned[group] * basins + basin)
+        for group in range(groups)
+        for basin in range(basins)
+    ]
+    received = lax.ppermute(passed, ("order", "basin"), pairs)
+    return jnp.where(lax.axis_index("order") == section + 1, received, 0.0)
 
 
 def per_device(
@@ -247,47 +279,53 @@
         received = lax.all_to_all(outgoing, "basin", split_axis=1, concat_axis=1, tiled=True)
         return received.reshape(-1, slots)
 
-    params = jnp.stack([travel_time, weight_x])
-    drain = jnp.stack([drain_basin[:, 0], drain_reach[:, 0]])
-    runoff, coefficients, send_table, outgoing = call(
+    def row(values):
+        return values.reshape(1, -1)
+
+    operands = (
+        forcings.reshape(days * channels, reaches),
+        w_input.T,
+        w_recur,
+        row(gate_bias),
+        row(w_runoff),
+        row(travel_time),
+        row(weight_x),
+        row(drain_basin),
+        row(drain_reach),
+    )
+    runoff, coefficients, send_table, targets = call(
         functools.partial(first_body, days=days, basins=basins),
         [
             series(),
             jax.ShapeDtypeStruct((3, reaches), F32),
             jax.ShapeDtypeStruct((reaches, slots), BF16),
-            payload(days + ID_ROWS),
+            jax.ShapeDtypeStruct((ID_ROWS, slots), F32),
         ],
-        megabytes=24,
-        scratch_shapes=[
+        megabytes=56,
+        in_specs=[pl.BlockSpec(memory_space=pltpu.HBM) for _ in operands],
+        scratch_shapes=[pltpu.VMEM(array.shape, array.dtype) for array in operands]
+        + [
             pltpu.VMEM((units // channels, 2 * units, 4 * units), BF16),
             pltpu.VMEM((reaches, units), F32),
+            pltpu.SemaphoreType.DMA((len(operands),)),
         ],
-    )(
-        forcings.reshape(days * channels, reaches),
-        w_input,
-        w_recur,
-        gate_bias[None, :],
-        w_runoff[None, :],
-        params,
-        drain,
-    )
-    arrivals = []
-    recv_table = None
+    )(*operands)
+
+    def send(arrive):
+        outgoing = call(pack_body, payload(days + ID_ROWS))(
+            runoff, coefficients, send_table, targets, arrive
+        )
+        return call(unpack_body, series())(exchange(outgoing))
+
+    def stay(arrive):
+        return jnp.zeros_like(arrive)
+
+    group = lax.axis_index("order")
+    arrive = jnp.zeros((days, reaches), F32)
     for section in range(groups - 1):
-        if section > 0:
-            outgoing = call(pack_body, payload(days))(runoff, coefficients, send_table, *arrivals)
-        received = exchange(outgoing)
-        if section == 0:
-            arrive, recv_table = call(
-                first_unpack_body, [series(), jax.ShapeDtypeStruct((slots, reaches), BF16)]
-            )(received)
-        else:
-            arrive = call(unpack_body, series())(received, recv_table)
-        pairs = [
-            (section * basins + basin, (section + 1) * basins + basin) for basin in range(basins)
-        ]
-        arrivals.append(lax.ppermute(arrive, ("order", "basin"), pairs))
-    return call(last_body, series())(runoff, coefficients, *arrivals)
+        passed = lax.cond(group == section, send, stay, arrive)
+        arrive = arrive + handed_on(passed, section, groups, basins)
+    return call(last_body, series())(runoff, coefficients, arrive)
 
 
 def solution(mesh):

time: 57.7 us -> 50.2 us (0.87)
  starting transfers between devices: 2.66 us -> 35.8 us
  blocking collectives: 29.9 us -> 0 us
  waiting for transfers between devices: 9.23 us -> 3.75 us
  local copies, waits for them, and re-layouts: 3.95 us -> 0.02 us
  Pallas kernels: 11.4 us -> 10.4 us
    ppermute x3, starting transfers between devices: 2.66 us -> 35.8 us  [handed_on(): received = lax.ppermute(passed, ('order', 'basin'), pairs)]
    all_to_all x3 -> x0, blocking collectives: 29.9 us -> none  [exchange(): lax.all_to_all(outgoing, 'basin', split_axis=0, concat_axis=0, tiled=True)]
    ppermute x3, waiting for transfers between devices: 9.23 us -> 3.75 us  [handed_on(): received = lax.ppermute(passed, ('order', 'basin'), pairs)]
    unnamed x17 -> x0, local copies, waits for them, and re-layouts: 3.95 us -> none
    pallas_call x6 -> x1, Pallas kernels: 2.43 us -> 0.7 us  [per_device(): return call(last_body, series())(runoff, coefficients, arrive)]
    pallas_call x1, Pallas kernels: 8.96 us -> 9.66 us  [per_device(): call(functools.partial(first_body, days=days, basins=basins), [series(),...]
  transfers between devices with their start and end apart: 3 -> 3, of which waited for: 1 -> 3; matrix products, arithmetic and copies ran while one was open for 0% -> 0% of each run, Pallas kernels for 0% -> 0%
where the time goes in v1:
time: 50.2 us; the launch traced here: 50 us
  starting transfers between devices  35.8 us (71%)
  Pallas kernels  10.4 us (21%)
  waiting for transfers between devices  3.75 us (7%)
    ppermute x3, starting transfers between devices, handed_on(): received = lax.ppermute(passed, ('order', 'basin'), pairs)  35.8 us
    pallas_call x1, Pallas kernels, per_device(): call(functools.partial(first_body, days=days, basins=basins), [series(),...  9.66 us
    ppermute x3, waiting for transfers between devices, handed_on(): received = lax.ppermute(passed, ('order', 'basin'), pairs)  3.75 us
  transfers between devices with their start and end apart: 3, of which 3 were waited for; matrix products, arithmetic and copies ran while one was open for 0% of the time, Pallas kernels for 0%

profile of v1, /device:TPU:5, one launch (start us, length us, event | category | flops | bytes accessed | tf_op | source)
XLA Modules:
  0.0 50.0 jit_solution(15424541038486473498)
XLA Ops:
  0.0 9.7 %shard_map.91 = (f32[32,512]{1,0:T(8,128)S(1)}, f32[3,512]{1,0:T(4,128)S(1)}, bf16[512,1024]{1,0:T(8,128)(2,1)S(1)}, f32[8,1024]{1,0:T(8,128)S(1)}) custom-call(bf16[512,512]{1,0:T(8,128)(2,1)} %bitcast.8, bf16[16,512]{1,0:T(8,128)(2,1)} %bitcast.9, bf16[512,128]{1,0:T(8,128)(2,1)} %w_recur_hbm.1, f32[1,512]{1,0:T(1,128)} %bitcast.10, f32[1,128]{1,0:T(1,128)} %bitcast.15, ...), custom_call_target="tpu_custom_call" | custom-call | tf_op jit(solution)/shard_map/pallas_call | solution.py:296
  9.7 0.7 %collective-permute-start = (f32[32,512]{1,0:T(8,128)S(1)}, f32[32,512]{1,0:T(8,128)S(1)}, u32[]{:S(2)}, u32[]{:S(2)}) collective-permute-start(f32[32,512]{1,0:T(8,128)S(1)} %get-tuple-element.64), channel_id=1, source_target_pairs={{0,8},{1,9},{2,10},{3,11},{4,12},{5,13},{6,14},{7,15},{8,0},{9,1},... | collective-permute-start | bytes 196616 | tf_op jit(solution)/shard_map/ppermute | solution.py:254
  10.4 0.9 %collective-permute-done = f32[32,512]{1,0:T(8,128)S(1)} collective-permute-done((f32[32,512]{1,0:T(8,128)S(1)}, f32[32,512]{1,0:T(8,128)S(1)}, u32[]{:S(2)}, u32[]{:S(2)}) %collective-permute-start) | collective-permute-done | bytes 65568 | tf_op jit(solution)/shard_map/ppermute | solution.py:254
  11.3 14.5 %collective-permute-start.1 = (f32[32,512]{1,0:T(8,128)S(1)}, f32[32,512]{1,0:T(8,128)S(1)}, u32[]{:S(2)}, u32[]{:S(2)}) collective-permute-start(f32[32,512]{1,0:T(8,128)S(1)} %get-tuple-element.65), channel_id=1, source_target_pairs={{0,24},{1,25},{2,26},{3,27},{4,28},{5,29},{6,30},{7,31},{8,16},{9,... | collective-permute-start | bytes 196616 | tf_op jit(solution)/shard_map/ppermute | solution.py:254
  25.9 2.0 %collective-permute-done.1 = f32[32,512]{1,0:T(8,128)S(1)} collective-permute-done((f32[32,512]{1,0:T(8,128)S(1)}, f32[32,512]{1,0:T(8,128)S(1)}, u32[]{:S(2)}, u32[]{:S(2)}) %collective-permute-start.1) | collective-permute-done | bytes 65568 | tf_op jit(solution)/shard_map/ppermute | solution.py:254
  27.9 20.5 %collective-permute-start.2 = (f32[32,512]{1,0:T(8,128)S(1)}, f32[32,512]{1,0:T(8,128)S(1)}, u32[]{:S(2)}, u32[]{:S(2)}) collective-permute-start(f32[32,512]{1,0:T(8,128)S(1)} %get-tuple-element.66), channel_id=1, source_target_pairs={{0,8},{1,9},{2,10},{3,11},{4,12},{5,13},{6,14},{7,15},{8,0},{9,1},... | collective-permute-start | bytes 196616 | tf_op jit(solution)/shard_map/ppermute | solution.py:254
  48.4 0.9 %collective-permute-done.2 = f32[32,512]{1,0:T(8,128)S(1)} collective-permute-done((f32[32,512]{1,0:T(8,128)S(1)}, f32[32,512]{1,0:T(8,128)S(1)}, u32[]{:S(2)}, u32[]{:S(2)}) %collective-permute-start.2) | collective-permute-done | bytes 65568 | tf_op jit(solution)/shard_map/ppermute | solution.py:254
  49.3 0.7 %shard_map.92 = f32[32,512]{1,0:T(8,128)} custom-call(f32[32,512]{1,0:T(8,128)S(1)} %get-tuple-element.60.runoff_ref, f32[3,512]{1,0:T(4,128)S(1)} %get-tuple-element.61.coefficients_ref, f32[32,512]{1,0:T(8,128)S(1)} %select_add_fusion.arrive_ref), custom_call_target="tpu_custom_call" | custom-call | tf_op jit(solution)/shard_map/pallas_call | solution.py:328
  (9 shorter events, 0.1 us)
Async XLA Ops:
  9.7 1.6 %collective-permute-start = (f32[32,512]{1,0:T(8,128)S(1)}, f32[32,512]{1,0:T(8,128)S(1)}, u32[]{:S(2)}, u32[]{:S(2)}) collective-permute-start(f32[32,512]{1,0:T(8,128)S(1)} %get-tuple-element.64), channel_id=1, source_target_pairs={{0,8},{1,9},{2,10},{3,11},{4,12},{5,13},{6,14},{7,15},{8,0},{9,1},... | collective-permute-start | bytes 196616 | tf_op jit(solution)/shard_map/ppermute | solution.py:254
  11.3 16.5 %collective-permute-start.1 = (f32[32,512]{1,0:T(8,128)S(1)}, f32[32,512]{1,0:T(8,128)S(1)}, u32[]{:S(2)}, u32[]{:S(2)}) collective-permute-start(f32[32,512]{1,0:T(8,128)S(1)} %get-tuple-element.65), channel_id=1, source_target_pairs={{0,24},{1,25},{2,26},{3,27},{4,28},{5,29},{6,30},{7,31},{8,16},{9,... | collective-permute-start | bytes 196616 | tf_op jit(solution)/shard_map/ppermute | solution.py:254
  27.9 21.4 %collective-permute-start.2 = (f32[32,512]{1,0:T(8,128)S(1)}, f32[32,512]{1,0:T(8,128)S(1)}, u32[]{:S(2)}, u32[]{:S(2)}) collective-permute-start(f32[32,512]{1,0:T(8,128)S(1)} %get-tuple-element.66), channel_id=1, source_target_pairs={{0,8},{1,9},{2,10},{3,11},{4,12},{5,13},{6,14},{7,15},{8,0},{9,1},... | collective-permute-start | bytes 196616 | tf_op jit(solution)/shard_map/ppermute | solution.py:254

commit v2 on v1

--- a/solution.py
+++ b/solution.py
@@ -10,6 +10,8 @@
 F32 = jnp.float32
 BF16 = jnp.bfloat16
 ID_ROWS = 8
+TABLE_ROWS = 16
+INFO_ROWS = 8
 CHUNK = 256
 
 
@@ -113,9 +115,13 @@
     drain_basin_hbm,
     drain_reach_hbm,
     runoff_ref,
-    coefficients_ref,
+    info_ref,
+    told_ref,
+    blank_ready_ref,
+    blank_table_ref,
     send_table_ref,
     targets_ref,
+    outgoing_ref,
     forcings_ref,
     w_input_ref,
     w_recur_ref,
@@ -177,12 +183,16 @@
     lane = lax.broadcasted_iota(jnp.int32, (chunk, units), 1)
 
     coefficients = routing_coefficients(travel_ref[...], weight_ref[...])
-    for row in range(3):
-        coefficients_ref[row : row + 1, :] = coefficients[row]
+    reach = drain_reach_ref[...]
+    known = (drain_basin_ref[...].astype(F32), reach.astype(F32)) + coefficients
+    for row, values in enumerate(known):
+        info_ref[row : row + 1, :] = values
+    info_ref[len(known) :, :] = jnp.zeros((INFO_ROWS - len(known), reaches), F32)
+    blank_ready_ref[...] = jnp.zeros_like(blank_ready_ref)
+    blank_table_ref[...] = jnp.zeros_like(blank_table_ref)
     slots = send_slots(drain_basin_ref[...], basins, capacity)
     send_table = one_hot(as_column(slots), basins * capacity)
     send_table_ref[...] = send_table
-    reach = drain_reach_ref[...]
     digits = jnp.concatenate([reach // 16, reach % 16, jnp.zeros((6, reaches), jnp.int32)], axis=0)
     found = jnp.dot(digits.astype(F32).astype(BF16), send_table, preferred_element_type=F32)
     targets_ref[...] = jnp.broadcast_to(16.0 * found[0:1] + found[1:2], targets_ref.shape)
@@ -220,10 +230,19 @@
     pre = jnp.transpose(sums[...])[:days]
     runoff = jnp.maximum(pre, 0.0) + jnp.log1p(jnp.exp(-jnp.abs(pre)))
     runoff_ref[...] = runoff
-
-
-def pack_body(runoff_ref, coefficients_ref, send_table_ref, targets_ref, arrive_ref, outgoing_ref):
-    routed = route(runoff_ref[...] + arrive_ref[...], coefficient_rows(coefficients_ref))
+    routed = route(runoff, coefficients)
+    told_ref[:days] = routed
+    told_ref[days:] = info_ref[...]
+    lay_out(outgoing_ref, choose(routed, send_table_ref[...]))
+    lay_out(outgoing_ref, targets_ref[...], days)
+
+
+def info_coefficients(ref):
+    return tuple(ref[row : row + 1, :] for row in range(2, 5))
+
+
+def pack_body(runoff_ref, info_ref, send_table_ref, targets_ref, arrive_ref, outgoing_ref):
+    routed = route(runoff_ref[...] + arrive_ref[...], info_coefficients(info_ref))
     lay_out(outgoing_ref, choose(routed, send_table_ref[...]))
     lay_out(outgoing_ref, targets_ref[...], routed.shape[0])
 
@@ -234,25 +253,93 @@
     arrive_ref[...] = choose(take_in(received_ref, 0, days), recv_table)
 
 
-def last_body(runoff_ref, coefficients_ref, arrive_ref, out_ref):
-    out_ref[...] = route(
-        runoff_ref[...] + arrive_ref[...], coefficient_rows(coefficients_ref)
-    )
-
-
-def coefficient_rows(ref):
-    return tuple(ref[row : row + 1, :] for row in range(3))
-
-
-def handed_on(passed, section, groups, basins):
-    turned = [(2 * section + 1 - group) % groups for group in range(groups)]
-    pairs = [
-        (group * basins + basin, turned[group] * basins + basin)
-        for group in range(groups)
-        for basin in range(basins)
+def pass_body(runoff_ref, info_ref, arrive_ref, out_ref):
+    days = runoff_ref.shape[0]
+    route_body(runoff_ref, info_ref, arrive_ref, out_ref.at[:days])
+    out_ref[days:] = info_ref[...]
+
+
+def route_body(runoff_ref, info_ref, arrive_ref, out_ref):
+    out_ref[...] = route(runoff_ref[...] + arrive_ref[...], info_coefficients(info_ref))
+
+
+def in_thirds(values):
+    high = values.astype(BF16)
+    rest = values - high.astype(F32)
+    middle = rest.astype(BF16)
+    return [high, middle, (rest - middle.astype(F32)).astype(BF16)]
+
+
+def spread_body(told_ref, out_ref):
+    for basin in range(out_ref.shape[0]):
+        out_ref[basin] = told_ref[told_ref.shape[0] - INFO_ROWS :, :]
+
+
+def info_table(tables_ref):
+    pieces = []
+    for basin in range(tables_ref.shape[0]):
+        reach = tables_ref[basin, 1:2, :].astype(jnp.int32)
+        rows = [tables_ref[basin, 0:1, :], (reach // 16).astype(F32), (reach % 16).astype(F32)]
+        for row in range(2, 5):
+            rows += [third.astype(F32) for third in in_thirds(tables_ref[basin, row : row + 1, :])]
+        rows.append(jnp.zeros((TABLE_ROWS - len(rows), reach.shape[1]), F32))
+        pieces.append(jnp.concatenate(rows, axis=0).astype(BF16))
+    return jnp.concatenate(pieces, axis=0)
+
+
+def looked_up(table, from_basin, from_reach):
+    reaches = table.shape[1]
+    sublanes = lax.broadcasted_iota(jnp.int32, (reaches, reaches), 0).astype(F32)
+    pick = jnp.where(sublanes == from_reach, 1.0, 0.0).astype(BF16)
+    picked = jnp.dot(table, pick, preferred_element_type=F32)
+    found = jnp.zeros((TABLE_ROWS, reaches), F32)
+    for basin in range(table.shape[0] // TABLE_ROWS):
+        here = from_basin == float(basin)
+        found = found + jnp.where(here, picked[basin * TABLE_ROWS : (basin + 1) * TABLE_ROWS], 0.0)
+    coefficients = tuple(
+        (found[row : row + 1] + found[row + 1 : row + 2]) + found[row + 2 : row + 3]
+        for row in (3, 6, 9)
+    )
+    return found[0:1], 16.0 * found[1:2] + found[2:3], coefficients
+
+
+def by_target(values, to_basin, to_reach, basins):
+    days, reaches = values.shape
+    halves = in_halves(values).astype(F32)
+    parts = [
+        jnp.where(to_basin == float(basin), halves, 0.0).astype(BF16) for basin in range(basins)
     ]
-    received = lax.ppermute(passed, ("order", "basin"), pairs)
-    return jnp.where(lax.axis_index("order") == section + 1, received, 0.0)
+    table = one_hot(as_column(to_reach), reaches)
+    sums = jnp.dot(jnp.concatenate(parts, axis=0), table, preferred_element_type=F32)
+    return [
+        sums[first : first + days] + sums[first + days : first + 2 * days]
+        for first in range(0, 2 * basins * days, 2 * days)
+    ]
+
+
+def prepare_body(before_ref, tables_ref, ready_ref, table_ref):
+    basins, days, _ = ready_ref.shape
+    table_ref[...] = info_table(tables_ref)
+    to_basin, to_reach = before_ref[days : days + 1, :], before_ref[days + 1 : days + 2, :]
+    for basin, sums in enumerate(by_target(before_ref[:days, :], to_basin, to_reach, basins)):
+        ready_ref[basin] = sums
+
+
+def pack_beyond_body(passed_ref, ready_ref, table_ref, outgoing_ref):
+    basins, days, _ = outgoing_ref.shape
+    to_basin, to_reach, coefficients = looked_up(
+        table_ref[...], passed_ref[days : days + 1, :], passed_ref[days + 1 : days + 2, :]
+    )
+    routed = route(passed_ref[:days, :], coefficients)
+    for basin, sums in enumerate(by_target(routed, to_basin, to_reach, basins)):
+        outgoing_ref[basin] = ready_ref[basin] + sums
+
+
+def add_up_body(received_ref, arrive_ref):
+    total = received_ref[0]
+    for basin in range(1, received_ref.shape[0]):
+        total = total + received_ref[basin]
+    arrive_ref[...] = total
 
 
 def per_device(
@@ -266,15 +353,15 @@
     slots = basins * capacity
     split = capacity % 128 == 0
 
-    def payload(rows):
-        return jax.ShapeDtypeStruct((basins, rows, capacity) if split else (rows, slots), F32)
-
     def series():
         return jax.ShapeDtypeStruct((days, reaches), F32)
 
+    def swap(outgoing):
+        return lax.all_to_all(outgoing, "basin", split_axis=0, concat_axis=0, tiled=True)
+
     def exchange(outgoing):
         if split:
-            return lax.all_to_all(outgoing, "basin", split_axis=0, concat_axis=0, tiled=True)
+            return swap(outgoing)
         outgoing = outgoing.reshape(-1, basins, capacity)
         received = lax.all_to_all(outgoing, "basin", split_axis=1, concat_axis=1, tiled=True)
         return received.reshape(-1, slots)
@@ -293,13 +380,24 @@
         row(drain_basin),
         row(drain_reach),
     )
-    runoff, coefficients, send_table, targets = call(
+    info_shape = jax.ShapeDtypeStruct((INFO_ROWS, reaches), F32)
+    told_shape = jax.ShapeDtypeStruct((days + INFO_ROWS, reaches), F32)
+    ready_shape = jax.ShapeDtypeStruct((basins, days, reaches), F32)
+    table_shape = jax.ShapeDtypeStruct((basins * TABLE_ROWS, reaches), BF16)
+    payload_shape = jax.ShapeDtypeStruct(
+        (basins, days + ID_ROWS, capacity) if split else (days + ID_ROWS, slots), F32
+    )
+    runoff, info, told, ready, table, send_table, targets, outgoing = call(
         functools.partial(first_body, days=days, basins=basins),
         [
             series(),
-            jax.ShapeDtypeStruct((3, reaches), F32),
+            info_shape,
+            told_shape,
+            ready_shape,
+            table_shape,
             jax.ShapeDtypeStruct((reaches, slots), BF16),
             jax.ShapeDtypeStruct((ID_ROWS, slots), F32),
+            payload_shape,
         ],
         megabytes=56,
         in_specs=[pl.BlockSpec(memory_space=pltpu.HBM) for _ in operands],
@@ -311,21 +409,79 @@
         ],
     )(*operands)
 
-    def send(arrive):
-        outgoing = call(pack_body, payload(days + ID_ROWS))(
-            runoff, coefficients, send_table, targets, arrive
+    group = lax.axis_index("order")
+    later = range(1, groups // 2)
+
+    def moved(block, routes):
+        pairs = [
+            (source * basins + basin, target * basins + basin)
+            for source, target in routes
+            for basin in range(basins)
+        ]
+        return lax.ppermute(block, ("order", "basin"), pairs)
+
+    neighbours = [(place, place ^ 1) for place in range(groups)]
+    two_down = [(place, (place + 2) % groups) for place in range(groups)]
+
+    def nothing(*_):
+        return jnp.zeros((days, reaches), F32)
+
+    def learn(told, ready, table):
+        before = moved(told, neighbours)
+
+        def prepare(before, ready, table):
+            spread = jax.ShapeDtypeStruct((basins, INFO_ROWS, reaches), F32)
+            tables = swap(call(spread_body, spread)(before))
+            return tuple(call(prepare_body, [ready_shape, table_shape], 24)(before, tables))
+
+        return lax.cond(
+            group % 2 == 1,
+            prepare,
+            lambda before, ready, table: (ready, table),
+            before,
+            ready,
+            table,
         )
+
+    ready, table = lax.cond(
+        group > 1, learn, lambda told, ready, table: (ready, table), told, ready, table
+    )
+    outgoing, ready, table = lax.optimization_barrier((outgoing, ready, table))
+
+    def deliver(outgoing):
         return call(unpack_body, series())(exchange(outgoing))
 
-    def stay(arrive):
-        return jnp.zeros_like(arrive)
-
-    group = lax.axis_index("order")
-    arrive = jnp.zeros((days, reaches), F32)
-    for section in range(groups - 1):
-        passed = lax.cond(group == section, send, stay, arrive)
-        arrive = arrive + handed_on(passed, section, groups, basins)
-    return call(last_body, series())(runoff, coefficients, arrive)
+    arrive = moved(lax.cond(group == 0, deliver, nothing, outgoing), neighbours)
+    arrive = jnp.where(group == 1, arrive, 0.0)
+    for pair in later:
+        above, between, below = 2 * pair - 1, 2 * pair, 2 * pair + 1
+        passed = moved(call(pass_body, told_shape)(runoff, info, arrive), two_down)
+        delivered = lax.cond(
+            group == above,
+            lambda arrive: deliver(
+                call(pack_body, payload_shape)(runoff, info, send_table, targets, arrive)
+            ),
+            nothing,
+            arrive,
+        )
+        passed, delivered = lax.optimization_barrier((passed, delivered))
+        received = lax.cond(
+            group == below,
+            lambda passed, _: call(add_up_body, series())(
+                swap(call(pack_beyond_body, ready_shape, 24)(passed, ready, table))
+            ),
+            lambda _, delivered: delivered,
+            passed,
+            delivered,
+        )
+        received = lax.cond(
+            (group == above) | (group == between),
+            lambda received: moved(received, [(above, between)]),
+            lambda received: received,
+            received,
+        )
+        arrive = arrive + jnp.where(group == above, 0.0, received)
+    return call(route_body, series())(runoff, info, arrive)
 
 
 def solution(mesh):

time: 50.2 us -> 42.8 us (0.85)
  starting transfers between devices: 35.8 us -> 1.1 us
  blocking collectives: 0 us -> 23.1 us
  waiting for transfers between devices: 3.75 us -> 5.84 us
  Pallas kernels: 10.4 us -> 12.4 us
    ppermute x3, starting transfers between devices: 35.8 us -> 1.1 us  [moved(): return lax.ppermute(block, ('order', 'basin'), pairs)]
    all_to_all x0 -> x2, blocking collectives: none -> 23.1 us  [swap(): lax.all_to_all(outgoing, 'basin', split_axis=0, concat_axis=0, tiled=True)]
    ppermute x3, waiting for transfers between devices: 3.75 us -> 5.84 us  [moved(): return lax.ppermute(block, ('order', 'basin'), pairs)]
    pallas_call x1 -> x6, Pallas kernels: 0.7 us -> 2.53 us  [the longest x1 0.96 us: per_device(): call(pack_beyond_body, ready_shape, 24)(passed, ready, table)]
where the time goes in v2:
time: 42.8 us; the launch traced here: 42.6 us
  blocking collectives  23.1 us (54%)
  Pallas kernels  12.4 us (29%)
  waiting for transfers between devices  5.84 us (14%)
  starting transfers between devices  1.1 us (3%)
    all_to_all x2, blocking collectives, swap(): lax.all_to_all(outgoing, 'basin', split_axis=0, concat_axis=0, tiled=True)  23.1 us
    pallas_call x1, Pallas kernels, per_device(): call(functools.partial(first_body, days=days, basins=basins), [series(),...  9.91 us
    ppermute x3, waiting for transfers between devices, moved(): return lax.ppermute(block, ('order', 'basin'), pairs)  5.84 us
    ppermute x3, starting transfers between devices, moved(): return lax.ppermute(block, ('order', 'basin'), pairs)  1.1 us
    pallas_call x1, Pallas kernels, per_device(): call(pack_beyond_body, ready_shape, 24)(passed, ready, table)  0.96 us
  transfers between devices with their start and end apart: 3, of which 3 were waited for; matrix products, arithmetic and copies ran while one was open for 0% of the time, Pallas kernels for 0%

profile of v2, /device:TPU:5, one launch (start us, length us, event | category | flops | bytes accessed | tf_op | source)
XLA Modules:
  0.0 42.6 jit_solution(10450315932906921608)
XLA Ops:
  0.0 9.9 %shard_map.91 = (f32[32,512]{1,0:T(8,128)S(1)}, f32[8,512]{1,0:T(8,128)S(1)}, f32[40,512]{1,0:T(8,128)S(1)}, f32[8,32,512]{2,1,0:T(8,128)S(1)}, bf16[128,512]{1,...) custom-call(bf16[512,512]{1,0:T(8,128)(2,1)} %bitcast.8, ...), custom_call_target="tpu_custom_call" | custom-call | tf_op jit(solution)/shard_map/pallas_call | solution.py:390
  9.9 14.0 %conditional.6 = ((f32[8,32,512]{2,1,0:T(8,128)S(1)}, bf16[128,512]{1,0:T(8,128)(2,1)S(1)})) conditional(s32[]{:T(128)} %convert_element_type.19, (f32[8,32,512]{2,1,0:T(8,128)S(1)}, bf16[128,512]{1,0:T(8,128)(2,1)S(1)}) %tuple.44, (s32[]{:T(128)}, f32[40,512]{1,0:T(8,128)S(1)}, f32[8,32,512]{2,1,0:T(8,128)S(1)}, bf16[128,512]{1,0:T(8,128)(2,1)S(1)}) %tuple.45), branch_computations={%region_0.0_spmd, %region_1.4_spmd} | conditional | flops 13 | bytes 590011 | solution.py:446
  9.9 0.8 %collective-permute-start = (f32[40,512]{1,0:T(8,128)S(1)}, f32[40,512]{1,0:T(8,128)S(1)}, u32[]{:S(2)}, u32[]{:S(2)}) collective-permute-start(f32[40,512]{1,0:T(8,128)S(1)} %get-tuple-element.57), channel_id=1, source_target_pairs={{0,8},{1,9},{2,10},{3,11},{4,12},{5,13},{6,14},{7,15},{8,0},{9,1},... | collective-permute-start | bytes 245768 | tf_op jit(solution)/shard_map/cond/branch_1_fun/ppermute | solution.py:421
  10.7 0.9 %collective-permute-done = f32[40,512]{1,0:T(8,128)S(1)} collective-permute-done((f32[40,512]{1,0:T(8,128)S(1)}, f32[40,512]{1,0:T(8,128)S(1)}, u32[]{:S(2)}, u32[]{:S(2)}) %collective-permute-start) | collective-permute-done | bytes 81952 | tf_op jit(solution)/shard_map/cond/branch_1_fun/ppermute | solution.py:421
  11.6 12.3 %conditional = ((f32[8,32,512]{2,1,0:T(8,128)S(1)}, bf16[128,512]{1,0:T(8,128)(2,1)S(1)})) conditional(s32[]{:T(128)} %convert_element_type.12, (f32[8,32,512]{2,1,0:T(8,128)S(1)}, bf16[128,512]{1,0:T(8,128)(2,1)S(1)}) %tuple.34, f32[40,512]{1,0:T(8,128)S(1)} %collective-permute-done), branch_computations={%region_2.2_spmd, %region_3.3_spmd} | conditional | bytes 262152 | solution.py:437
  11.6 11.5 %all_to_all.16.tables_ref = f32[8,8,512]{2,1,0:T(8,128)S(1)} all-to-all(f32[8,8,512]{2,1,0:T(8,128)S(1)} %branch_1_fun.7), channel_id=1, replica_groups=mesh['order'=4,'basin'=8] {'basin'}, dimensions={0} | all-to-all | bytes 262144 | tf_op jit(solution)/shard_map/cond/branch_1_fun/cond/branch_1_fun/all_to_all | solution.py:360
  23.1 0.8 %branch_1_fun.8 = (f32[8,32,512]{2,1,0:T(8,128)S(1)}, bf16[128,512]{1,0:T(8,128)(2,1)S(1)}) custom-call(f32[40,512]{1,0:T(8,128)S(1)} %before_ref, f32[8,8,512]{2,1,0:T(8,128)S(1)} %all_to_all.16.tables_ref), custom_call_target="tpu_custom_call" | custom-call | tf_op jit(solution)/shard_map/cond/branch_1_fun/cond/branch_1_fun/pallas_call | solution.py:435
  24.0 0.1 collective-permute-start.2
  24.0 1.2 %collective-permute-done.2 = f32[32,512]{1,0:T(8,128)S(1)} collective-permute-done((f32[32,512]{1,0:T(8,128)S(1)}, f32[32,512]{1,0:T(8,128)S(1)}, u32[]{:S(2)}, u32[]{:S(2)}) %collective-permute-start.2) | collective-permute-done | bytes 65568 | tf_op jit(solution)/shard_map/ppermute | solution.py:421
  25.3 0.1 shard_map.92
  25.4 0.3 collective-permute-start.3
  25.6 3.7 %collective-permute-done.3 = f32[40,512]{1,0:T(8,128)S(1)} collective-permute-done((f32[40,512]{1,0:T(8,128)S(1)}, f32[40,512]{1,0:T(8,128)S(1)}, u32[]{:S(2)}, u32[]{:S(2)}) %collective-permute-start.3) | collective-permute-done | bytes 81952 | tf_op jit(solution)/shard_map/ppermute | solution.py:421
  29.3 12.6 %conditional.9 = (f32[32,512]{1,0:T(8,128)S(1)}) conditional(s32[]{:T(128)} %convert_element_type.21, f32[32,512]{1,0:T(8,128)S(1)} %get-tuple-element.107, (f32[40,512]{1,0:T(8,128)S(1)}, f32[8,32,512]{2,1,0:T(8,128)S(1)}, bf16[128,512]{1,0:T(8,128)(2,1)S(1)}) %tuple.50), branch_computations={%region_8.9_spmd, %region_9.10_spmd} | conditional | bytes 1048584 | solution.py:468
  29.3 1.0 %branch_1_fun.12 = f32[8,32,512]{2,1,0:T(8,128)S(1)} custom-call(f32[40,512]{1,0:T(8,128)S(1)} %get-tuple-element.63.passed_ref, f32[8,32,512]{2,1,0:T(8,128)S(1)} %get-tuple-element.64.ready_ref, bf16[128,512]{1,0:T(8,128)(2,1)S(1)} %get-tuple-element.65.table_ref), custom_call_target="tpu_custom_call" | custom-call | tf_op jit(solution)/shard_map/cond/branch_1_fun/pallas_call | solution.py:471
  30.3 11.6 %all_to_all.19.received_ref = f32[8,32,512]{2,1,0:T(8,128)S(1)} all-to-all(f32[8,32,512]{2,1,0:T(8,128)S(1)} %branch_1_fun.12), channel_id=1, replica_groups=mesh['order'=4,'basin'=8] {'basin'}, dimensions={0} | all-to-all | bytes 1048576 | tf_op jit(solution)/shard_map/cond/branch_1_fun/all_to_all | solution.py:360
  42.0 0.7 %shard_map.93 = f32[32,512]{1,0:T(8,128)} custom-call(f32[32,512]{1,0:T(8,128)S(1)} %get-tuple-element.81.runoff_ref, f32[8,512]{1,0:T(8,128)S(1)} %get-tuple-element.82.info_ref, f32[32,512]{1,0:T(8,128)S(1)} %select_add_fusion.arrive_ref), custom_call_target="tpu_custom_call" | custom-call | tf_op jit(solution)/shard_map/pallas_call | solution.py:484
  (9 shorter events, 0.1 us)
Async XLA Ops:
  9.9 1.7 %collective-permute-start = (f32[40,512]{1,0:T(8,128)S(1)}, f32[40,512]{1,0:T(8,128)S(1)}, u32[]{:S(2)}, u32[]{:S(2)}) collective-permute-start(f32[40,512]{1,0:T(8,128)S(1)} %get-tuple-element.57), channel_id=1, source_target_pairs={{0,8},{1,9},{2,10},{3,11},{4,12},{5,13},{6,14},{7,15},{8,0},{9,1},... | collective-permute-start | bytes 245768 | tf_op jit(solution)/shard_map/cond/branch_1_fun/ppermute | solution.py:421
  24.0 1.3 %collective-permute-start.2 = (f32[32,512]{1,0:T(8,128)S(1)}, f32[32,512]{1,0:T(8,128)S(1)}, u32[]{:S(2)}, u32[]{:S(2)}) collective-permute-start(f32[32,512]{1,0:T(8,128)S(1)} %get-tuple-element.106), channel_id=1, source_target_pairs={{0,8},{1,9},{2,10},{3,11},{4,12},{5,13},{6,14},{7,15},{8,0},{9,1},... | collective-permute-start | bytes 196616 | tf_op jit(solution)/shard_map/ppermute | solution.py:421
  25.4 4.0 %collective-permute-start.3 = (f32[40,512]{1,0:T(8,128)S(1)}, f32[40,512]{1,0:T(8,128)S(1)}, u32[]{:S(2)}, u32[]{:S(2)}) collective-permute-start(f32[40,512]{1,0:T(8,128)S(1)} %shard_map.92), channel_id=1, source_target_pairs={{0,16},{1,17},{2,18},{3,19},{4,20},{5,21},{6,22},{7,23},{8,24},{9,... | collective-permute-start | bytes 245768 | tf_op jit(solution)/shard_map/ppermute | solution.py:421

commit v3 on v2

--- a/solution.py
+++ b/solution.py
@@ -11,8 +11,9 @@
 BF16 = jnp.bfloat16
 ID_ROWS = 8
 TABLE_ROWS = 16
+KNOWN = 5
 INFO_ROWS = 8
-CHUNK = 256
+CHUNK = 512
 
 
 def vmem():
@@ -102,6 +103,28 @@
     earlier = jnp.dot(member.astype(BF16), upper, preferred_element_type=F32)
     rank = jnp.sum(member * earlier, axis=0, keepdims=True)
     return drain_to.astype(F32) * capacity + rank
+
+
+def slot_tables(drain_to, reach, basins, capacity):
+    send_table = one_hot(as_column(send_slots(drain_to, basins, capacity)), basins * capacity)
+    digits = jnp.concatenate(
+        [reach // 16, reach % 16, jnp.zeros((6, reach.shape[1]), jnp.int32)], axis=0
+    )
+    found = jnp.dot(digits.astype(F32).astype(BF16), send_table, preferred_element_type=F32)
+    return send_table, jnp.broadcast_to(
+        16.0 * found[0:1] + found[1:2], (ID_ROWS, send_table.shape[1])
+    )
+
+
+def known(drain_basin, drain_reach, travel_time, weight_x):
+    rows = (drain_basin.astype(F32), drain_reach.astype(F32))
+    rows += routing_coefficients(travel_time, weight_x)
+    blank = jnp.zeros((INFO_ROWS - len(rows), travel_time.shape[1]), F32)
+    return jnp.concatenate([*rows, blank], axis=0)
+
+
+def coefficients_of(info):
+    return tuple(info[row : row + 1, :] for row in range(2, KNOWN))
 
 
 def first_body(
@@ -115,10 +138,14 @@
     drain_basin_hbm,
     drain_reach_hbm,
     runoff_ref,
-    info_ref,
     told_ref,
-    blank_ready_ref,
-    blank_table_ref,
+    spread_ref,
+    between_ref,
+    above_ref,
+    ready_ref,
+    paths_ref,
+    missing_ref,
+    absent_ref,
     send_table_ref,
     targets_ref,
     outgoing_ref,
@@ -182,20 +209,15 @@
     chunks = reaches // chunk
     lane = lax.broadcasted_iota(jnp.int32, (chunk, units), 1)
 
-    coefficients = routing_coefficients(travel_ref[...], weight_ref[...])
-    reach = drain_reach_ref[...]
-    known = (drain_basin_ref[...].astype(F32), reach.astype(F32)) + coefficients
-    for row, values in enumerate(known):
-        info_ref[row : row + 1, :] = values
-    info_ref[len(known) :, :] = jnp.zeros((INFO_ROWS - len(known), reaches), F32)
-    blank_ready_ref[...] = jnp.zeros_like(blank_ready_ref)
-    blank_table_ref[...] = jnp.zeros_like(blank_table_ref)
-    slots = send_slots(drain_basin_ref[...], basins, capacity)
-    send_table = one_hot(as_column(slots), basins * capacity)
+    info = known(drain_basin_ref[...], drain_reach_ref[...], travel_ref[...], weight_ref[...])
+    told_ref[days:, :] = info
+    for basin in range(basins):
+        spread_ref[basin] = info
+    send_table, targets = slot_tables(drain_basin_ref[...], drain_reach_ref[...], basins, capacity)
     send_table_ref[...] = send_table
-    digits = jnp.concatenate([reach // 16, reach % 16, jnp.zeros((6, reaches), jnp.int32)], axis=0)
-    found = jnp.dot(digits.astype(F32).astype(BF16), send_table, preferred_element_type=F32)
-    targets_ref[...] = jnp.broadcast_to(16.0 * found[0:1] + found[1:2], targets_ref.shape)
+    targets_ref[...] = targets
+    for blank_ref in (between_ref, above_ref, ready_ref, paths_ref, missing_ref, absent_ref):
+        blank_ref[...] = jnp.zeros_like(blank_ref)
     loads[-1].wait()
 
     def block_of_days(block, state):
@@ -226,41 +248,35 @@
     state = tuple(
         (jnp.zeros((chunk, units), BF16), jnp.zeros((chunk, units), F32)) for _ in range(chunks)
     )
-    lax.fori_loop(0, days // per_block, block_of_days, state)
+    lax.fori_loop(0, days // per_block, block_of_days, state, unroll=True)
     pre = jnp.transpose(sums[...])[:days]
     runoff = jnp.maximum(pre, 0.0) + jnp.log1p(jnp.exp(-jnp.abs(pre)))
     runoff_ref[...] = runoff
-    routed = route(runoff, coefficients)
-    told_ref[:days] = routed
-    told_ref[days:] = info_ref[...]
+    routed = route(runoff, coefficients_of(info))
+    told_ref[:days, :] = routed
     lay_out(outgoing_ref, choose(routed, send_table_ref[...]))
     lay_out(outgoing_ref, targets_ref[...], days)
 
 
-def info_coefficients(ref):
-    return tuple(ref[row : row + 1, :] for row in range(2, 5))
-
-
-def pack_body(runoff_ref, info_ref, send_table_ref, targets_ref, arrive_ref, outgoing_ref):
-    routed = route(runoff_ref[...] + arrive_ref[...], info_coefficients(info_ref))
+def unpack_body(received_ref, *arrive_refs):
+    days, reaches = arrive_refs[0].shape
+    recv_table = one_hot(as_column(take_in(received_ref, days, 1)), reaches)
+    arrive = choose(take_in(received_ref, 0, days), recv_table)
+    for arrive_ref in arrive_refs:
+        arrive_ref[...] = arrive
+
+
+def route_body(runoff_ref, told_ref, arrive_ref, out_ref):
+    info = told_ref[runoff_ref.shape[0] :, :]
+    out_ref[...] = route(runoff_ref[...] + arrive_ref[...], coefficients_of(info))
+
+
+def pack_body(runoff_ref, told_ref, send_table_ref, targets_ref, arrive_ref, outgoing_ref):
+    days = runoff_ref.shape[0]
+    info = told_ref[days:, :]
+    routed = route(runoff_ref[...] + arrive_ref[...], coefficients_of(info))
     lay_out(outgoing_ref, choose(routed, send_table_ref[...]))
-    lay_out(outgoing_ref, targets_ref[...], routed.shape[0])
-
-
-def unpack_body(received_ref, arrive_ref):
-    days, reaches = arrive_ref.shape
-    recv_table = one_hot(as_column(take_in(received_ref, days, 1)), reaches)
-    arrive_ref[...] = choose(take_in(received_ref, 0, days), recv_table)
-
-
-def pass_body(runoff_ref, info_ref, arrive_ref, out_ref):
-    days = runoff_ref.shape[0]
-    route_body(runoff_ref, info_ref, arrive_ref, out_ref.at[:days])
-    out_ref[days:] = info_ref[...]
-
-
-def route_body(runoff_ref, info_ref, arrive_ref, out_ref):
-    out_ref[...] = route(runoff_ref[...] + arrive_ref[...], info_coefficients(info_ref))
+    lay_out(outgoing_ref, targets_ref[...], days)
 
 
 def in_thirds(values):
@@ -270,18 +286,22 @@
     return [high, middle, (rest - middle.astype(F32)).astype(BF16)]
 
 
-def spread_body(told_ref, out_ref):
-    for basin in range(out_ref.shape[0]):
-        out_ref[basin] = told_ref[told_ref.shape[0] - INFO_ROWS :, :]
-
-
-def info_table(tables_ref):
+def bundle_body(told_ref, tables_ref, bundle_ref):
+    rows = told_ref.shape[0]
+    bundle_ref[:rows, :] = told_ref[...]
+    for basin in range(tables_ref.shape[0]):
+        first = rows + basin * INFO_ROWS
+        bundle_ref[first : first + INFO_ROWS, :] = tables_ref[basin]
+
+
+def info_table(tables):
     pieces = []
-    for basin in range(tables_ref.shape[0]):
-        reach = tables_ref[basin, 1:2, :].astype(jnp.int32)
-        rows = [tables_ref[basin, 0:1, :], (reach // 16).astype(F32), (reach % 16).astype(F32)]
-        for row in range(2, 5):
-            rows += [third.astype(F32) for third in in_thirds(tables_ref[basin, row : row + 1, :])]
+    for first in range(0, tables.shape[0], INFO_ROWS):
+        info = tables[first : first + INFO_ROWS]
+        reach = info[1:2].astype(jnp.int32)
+        rows = [info[0:1], (reach // 16).astype(F32), (reach % 16).astype(F32)]
+        for row in range(2, KNOWN):
+            rows += [third.astype(F32) for third in in_thirds(info[row : row + 1])]
         rows.append(jnp.zeros((TABLE_ROWS - len(rows), reach.shape[1]), F32))
         pieces.append(jnp.concatenate(rows, axis=0).astype(BF16))
     return jnp.concatenate(pieces, axis=0)
@@ -317,21 +337,26 @@
     ]
 
 
-def prepare_body(before_ref, tables_ref, ready_ref, table_ref):
-    basins, days, _ = ready_ref.shape
-    table_ref[...] = info_table(tables_ref)
-    to_basin, to_reach = before_ref[days : days + 1, :], before_ref[days + 1 : days + 2, :]
-    for basin, sums in enumerate(by_target(before_ref[:days, :], to_basin, to_reach, basins)):
+def prepare_body(between_ref, above_ref, ready_ref, paths_ref):
+    basins, days, reaches = ready_ref.shape
+    rows = days + INFO_ROWS
+    to_basin, to_reach, coefficients = looked_up(
+        info_table(between_ref[rows:, :]), above_ref[days : days + 1, :], above_ref[days + 1 : days + 2, :]
+    )
+    paths_ref[:rows, :] = above_ref[...]
+    blank = jnp.zeros((INFO_ROWS - KNOWN, reaches), F32)
+    paths_ref[rows:, :] = jnp.concatenate([to_basin, to_reach, *coefficients, blank], axis=0)
+    own = between_ref[days:rows, :]
+    for basin, sums in enumerate(by_target(between_ref[:days, :], own[0:1], own[1:2], basins)):
         ready_ref[basin] = sums
 
 
-def pack_beyond_body(passed_ref, ready_ref, table_ref, outgoing_ref):
+def pack_beyond_body(passed_ref, ready_ref, paths_ref, outgoing_ref):
     basins, days, _ = outgoing_ref.shape
-    to_basin, to_reach, coefficients = looked_up(
-        table_ref[...], passed_ref[days : days + 1, :], passed_ref[days + 1 : days + 2, :]
-    )
-    routed = route(passed_ref[:days, :], coefficients)
-    for basin, sums in enumerate(by_target(routed, to_basin, to_reach, basins)):
+    above, between = paths_ref[days : days + INFO_ROWS, :], paths_ref[days + INFO_ROWS :, :]
+    outflow = paths_ref[:days, :] + route(passed_ref[...], coefficients_of(above))
+    routed = route(outflow, coefficients_of(between))
+    for basin, sums in enumerate(by_target(routed, between[0:1], between[1:2], basins)):
         outgoing_ref[basin] = ready_ref[basin] + sums
 
 
@@ -380,21 +405,25 @@
         row(drain_basin),
         row(drain_reach),
     )
-    info_shape = jax.ShapeDtypeStruct((INFO_ROWS, reaches), F32)
     told_shape = jax.ShapeDtypeStruct((days + INFO_ROWS, reaches), F32)
+    bundle_shape = jax.ShapeDtypeStruct((days + (1 + basins) * INFO_ROWS, reaches), F32)
     ready_shape = jax.ShapeDtypeStruct((basins, days, reaches), F32)
-    table_shape = jax.ShapeDtypeStruct((basins * TABLE_ROWS, reaches), BF16)
+    paths_shape = jax.ShapeDtypeStruct((days + 2 * INFO_ROWS, reaches), F32)
     payload_shape = jax.ShapeDtypeStruct(
         (basins, days + ID_ROWS, capacity) if split else (days + ID_ROWS, slots), F32
     )
-    runoff, info, told, ready, table, send_table, targets, outgoing = call(
+    runoff, told, spread, between, above, ready, paths, *late = call(
         functools.partial(first_body, days=days, basins=basins),
         [
             series(),
-            info_shape,
+            told_shape,
+            jax.ShapeDtypeStruct((basins, INFO_ROWS, reaches), F32),
+            bundle_shape,
             told_shape,
             ready_shape,
-            table_shape,
+            paths_shape,
+            series(),
+            series(),
             jax.ShapeDtypeStruct((reaches, slots), BF16),
             jax.ShapeDtypeStruct((ID_ROWS, slots), F32),
             payload_shape,
@@ -409,6 +438,7 @@
         ],
     )(*operands)
 
+    missing, absent, send_table, targets, outgoing = late
     group = lax.axis_index("order")
     later = range(1, groups // 2)
 
@@ -426,41 +456,59 @@
     def nothing(*_):
         return jnp.zeros((days, reaches), F32)
 
-    def learn(told, ready, table):
-        before = moved(told, neighbours)
-
-        def prepare(before, ready, table):
-            spread = jax.ShapeDtypeStruct((basins, INFO_ROWS, reaches), F32)
-            tables = swap(call(spread_body, spread)(before))
-            return tuple(call(prepare_body, [ready_shape, table_shape], 24)(before, tables))
-
-        return lax.cond(
-            group % 2 == 1,
-            prepare,
-            lambda before, ready, table: (ready, table),
-            before,
-            ready,
-            table,
-        )
-
-    ready, table = lax.cond(
-        group > 1, learn, lambda told, ready, table: (ready, table), told, ready, table
-    )
-    outgoing, ready, table = lax.optimization_barrier((outgoing, ready, table))
-
-    def deliver(outgoing):
-        return call(unpack_body, series())(exchange(outgoing))
-
-    arrive = moved(lax.cond(group == 0, deliver, nothing, outgoing), neighbours)
+    above = lax.cond(
+        group % 2 == 1, lambda told, blank: moved(told, two_down), lambda _, blank: blank, told, above
+    )
+    spread, above = lax.optimization_barrier((spread, above))
+    between = lax.cond(
+        (group % 2 == 0) & (group > 1),
+        lambda spread, told, _: call(bundle_body, bundle_shape)(told, swap(spread)),
+        lambda spread, told, blank: blank,
+        spread,
+        told,
+        between,
+    )
+    outgoing, between = lax.optimization_barrier((outgoing, between))
+
+    def deliver(outgoing, copies=1):
+        return tuple(call(unpack_body, [series()] * copies)(exchange(outgoing)))
+
+    arrive, passed = lax.cond(
+        group == 0,
+        lambda outgoing, *_: deliver(outgoing, 2),
+        lambda outgoing, *blanks: tuple(blanks),
+        outgoing,
+        missing,
+        absent,
+    )
+    arrive, passed, between = lax.optimization_barrier((arrive, passed, between))
+    passed = moved(passed, [(0, 3)] if groups > 3 else [])
+    between = lax.cond(
+        group > 1, lambda told: moved(told, neighbours), lambda told: told, between
+    )
+    ready, paths = lax.cond(
+        (group % 2 == 1) & (group > 1),
+        lambda *known: tuple(call(prepare_body, [ready_shape, paths_shape], 24)(*known[:2])),
+        lambda between, above, ready, paths: (ready, paths),
+        between,
+        above,
+        ready,
+        paths,
+    )
+    arrive, ready = lax.optimization_barrier((arrive, ready))
+    arrive = lax.cond(
+        group < 2, lambda arrive: moved(arrive, neighbours), lambda arrive: arrive, arrive
+    )
     arrive = jnp.where(group == 1, arrive, 0.0)
     for pair in later:
         above, between, below = 2 * pair - 1, 2 * pair, 2 * pair + 1
-        passed = moved(call(pass_body, told_shape)(runoff, info, arrive), two_down)
+        if pair > 1:
+            passed = moved(arrive, two_down)
         delivered = lax.cond(
             group == above,
             lambda arrive: deliver(
-                call(pack_body, payload_shape)(runoff, info, send_table, targets, arrive)
-            ),
+                call(pack_body, payload_shape)(runoff, told, send_table, targets, arrive)
+            )[0],
             nothing,
             arrive,
         )
@@ -468,7 +516,7 @@
         received = lax.cond(
             group == below,
             lambda passed, _: call(add_up_body, series())(
-                swap(call(pack_beyond_body, ready_shape, 24)(passed, ready, table))
+                swap(call(pack_beyond_body, ready_shape, 24)(passed, ready, paths))
             ),
             lambda _, delivered: delivered,
             passed,
@@ -481,7 +529,7 @@
             received,
         )
         arrive = arrive + jnp.where(group == above, 0.0, received)
-    return call(route_body, series())(runoff, info, arrive)
+    return call(route_body, series())(runoff, told, arrive)
 
 
 def solution(mesh):

time: 42.8 us -> 40 us (0.935)
  blocking collectives: 23.1 us -> 11.6 us
  starting transfers between devices: 1.1 us -> 11.1 us
  Pallas kernels: 12.4 us -> 11.1 us
    all_to_all x2 -> x1, blocking collectives: 23.1 us -> 11.6 us  [swap(): lax.all_to_all(outgoing, 'basin', split_axis=0, concat_axis=0, tiled=True)]
    ppermute x3, starting transfers between devices: 1.1 us -> 11.1 us  [moved(): return lax.ppermute(block, ('order', 'basin'), pairs)]
    pallas_call x1, Pallas kernels: 9.91 us -> 8.9 us  [per_device(): call(functools.partial(first_body, days=days, basins=basins), [series(),...]
    pallas_call x5 -> x3, Pallas kernels: 2.51 us -> 2.2 us  [the longest x1 0.79 us: per_device(): call(prepare_body, [ready_shape, paths_shape], 24)(*known[:2])]
  transfers between devices with their start and end apart: 3 -> 3, of which waited for: 3 -> 3; matrix products, arithmetic and copies ran while one was open for 0% -> 0% of each run, Pallas kernels for 0% -> 2%
where the time goes in v3:
time: 40 us; the launch traced here: 39.8 us
  blocking collectives  11.6 us (29%)
  Pallas kernels  11.1 us (28%)
  starting transfers between devices  11.1 us (28%)
  waiting for transfers between devices  5.68 us (14%)
    all_to_all x1, blocking collectives, swap(): lax.all_to_all(outgoing, 'basin', split_axis=0, concat_axis=0, tiled=True)  11.6 us
    ppermute x3, starting transfers between devices, moved(): return lax.ppermute(block, ('order', 'basin'), pairs)  11.1 us
    pallas_call x1, Pallas kernels, per_device(): call(functools.partial(first_body, days=days, basins=basins), [series(),...  8.9 us
    ppermute x3, waiting for transfers between devices, moved(): return lax.ppermute(block, ('order', 'basin'), pairs)  5.68 us
  transfers between devices with their start and end apart: 3, of which 3 were waited for; matrix products, arithmetic and copies ran while one was open for 0% of the time, Pallas kernels for 2%

profile of v3, /device:TPU:5, one launch (start us, length us, event | category | flops | bytes accessed | tf_op | source)
XLA Modules:
  0.0 39.8 jit_solution(14462390631123526111)
XLA Ops:
  0.0 8.9 %shard_map.91 = (f32[32,512]{1,0:T(8,128)S(1)}, f32[40,512]{1,0:T(8,128)S(1)}, f32[8,8,512]{2,1,0:T(8,128)S(1)}, f32[104,512]{1,0:T(8,128)S(1)}, f32[40,512]{1,0...) custom-call(bf16[512,512]{1,0:T(8,128)(2,1)} %bitcast.8, ...), custom_call_target="tpu_custom_call" | custom-call | tf_op jit(solution)/shard_map/pallas_call | solution.py:415
  8.9 3.4 %conditional.9 = (f32[40,512]{1,0:T(8,128)S(1)}) conditional(s32[]{:T(128)} %convert_element_type.30, f32[40,512]{1,0:T(8,128)S(1)} %get-tuple-element.115, f32[40,512]{1,0:T(8,128)S(1)} %get-tuple-element.109.told_ref), branch_computations={%region_0.1_spmd, %region_1.2_spmd} | conditional | bytes 491568 | solution.py:459
  8.9 0.1 collective-permute-start
  9.0 3.3 %collective-permute-done = f32[40,512]{1,0:T(8,128)S(1)} collective-permute-done((f32[40,512]{1,0:T(8,128)S(1)}, f32[40,512]{1,0:T(8,128)S(1)}, u32[]{:S(2)}, u32[]{:S(2)}) %collective-permute-start) | collective-permute-done | bytes 81952 | tf_op jit(solution)/shard_map/cond/branch_1_fun/ppermute | solution.py:451
  12.3 1.3 %collective-permute-start.4 = (f32[32,512]{1,0:T(8,128)S(1)}, f32[32,512]{1,0:T(8,128)S(1)}, u32[]{:S(2)}, u32[]{:S(2)}) collective-permute-start(f32[32,512]{1,0:T(8,128)S(1)} %get-tuple-element.128), channel_id=1, source_target_pairs={{0,24},{1,25},{2,26},{3,27},{4,28},{5,29},{6,30},{7,31}} | collective-permute-start | bytes 196616 | tf_op jit(solution)/shard_map/ppermute | solution.py:451
  13.6 10.8 %conditional.12 = (f32[104,512]{1,0:T(8,128)S(1)}) conditional(s32[]{:T(128)} %convert_element_type.32, f32[104,512]{1,0:T(8,128)S(1)} %get-tuple-element.144, f32[104,512]{1,0:T(8,128)S(1)} %get-tuple-element.144), branch_computations={%region_6.7_spmd, %region_7.8_spmd} | conditional | bytes 1278000 | solution.py:486
  13.6 9.7 %collective-permute-start.1 = (f32[104,512]{1,0:T(8,128)S(1)}, f32[104,512]{1,0:T(8,128)S(1)}, u32[]{:S(2)}, u32[]{:S(2)}) collective-permute-start(f32[104,512]{1,0:T(8,128)S(1)} %param.7), channel_id=1, source_target_pairs={{0,8},{1,9},{2,10},{3,11},{4,12},{5,13},{6,14},{7,15},{8,0},{9,1},... | collective-permute-start | bytes 638984 | tf_op jit(solution)/shard_map/cond/branch_1_fun/ppermute | solution.py:451
  23.4 1.1 %collective-permute-done.1 = f32[104,512]{1,0:T(8,128)S(1)} collective-permute-done((f32[104,512]{1,0:T(8,128)S(1)}, f32[104,512]{1,0:T(8,128)S(1)}, u32[]{:S(2)}, u32[]{:S(2)}) %collective-permute-start.1) | collective-permute-done | bytes 213024 | tf_op jit(solution)/shard_map/cond/branch_1_fun/ppermute | solution.py:451
  24.5 0.8 %conditional.13 = ((f32[8,32,512]{2,1,0:T(8,128)S(1)}, f32[48,512]{1,0:T(8,128)S(1)})) conditional(s32[]{:T(128)} %convert_element_type.31, (f32[8,32,512]{2,1,0:T(8,128)S(1)}, f32[48,512]{1,0:T(8,128)S(1)}) %tuple.69, (f32[104,512]{1,0:T(8,128)S(1)}, f32[40,512]{1,0:T(8,128)S(1)}) %tuple.70), branch_computations={%region_8.9_spmd, %region_9.10_spmd} | conditional | bytes 8 | solution.py:489
  24.5 0.8 %branch_1_fun.9 = (f32[8,32,512]{2,1,0:T(8,128)S(1)}, f32[48,512]{1,0:T(8,128)S(1)}) custom-call(f32[104,512]{1,0:T(8,128)S(1)} %get-tuple-element.71.between_ref, f32[40,512]{1,0:T(8,128)S(1)} %get-tuple-element.72.above_ref), custom_call_target="tpu_custom_call" | custom-call | tf_op jit(solution)/shard_map/cond/branch_1_fun/pallas_call | solution.py:491
  25.4 1.3 %collective-permute-done.4 = f32[32,512]{1,0:T(8,128)S(1)} collective-permute-done((f32[32,512]{1,0:T(8,128)S(1)}, f32[32,512]{1,0:T(8,128)S(1)}, u32[]{:S(2)}, u32[]{:S(2)}) %collective-permute-start.4) | collective-permute-done | bytes 65568 | tf_op jit(solution)/shard_map/ppermute | solution.py:451
  26.7 12.3 %conditional.16 = (f32[32,512]{1,0:T(8,128)S(1)}) conditional(s32[]{:T(128)} %convert_element_type.34, f32[32,512]{1,0:T(8,128)S(1)} %get-tuple-element.149, (f32[32,512]{1,0:T(8,128)S(1)}, f32[8,32,512]{2,1,0:T(8,128)S(1)}, f32[48,512]{1,0:T(8,128)S(1)}) %tuple.75), branch_computations={%region_14.15_spmd, %region_15.16_spmd} | conditional | bytes 1048584 | solution.py:516
  26.7 0.7 %branch_1_fun.12 = f32[8,32,512]{2,1,0:T(8,128)S(1)} custom-call(f32[32,512]{1,0:T(8,128)S(1)} %get-tuple-element.78.passed_ref, f32[8,32,512]{2,1,0:T(8,128)S(1)} %get-tuple-element.79.ready_ref, f32[48,512]{1,0:T(8,128)S(1)} %get-tuple-element.80.paths_ref), custom_call_target="tpu_custom_call" | custom-call | tf_op jit(solution)/shard_map/cond/branch_1_fun/pallas_call | solution.py:519
  27.4 11.6 %all_to_all.19.received_ref = f32[8,32,512]{2,1,0:T(8,128)S(1)} all-to-all(f32[8,32,512]{2,1,0:T(8,128)S(1)} %branch_1_fun.12), channel_id=1, replica_groups=mesh['order'=4,'basin'=8] {'basin'}, dimensions={0} | all-to-all | bytes 1048576 | tf_op jit(solution)/shard_map/cond/branch_1_fun/all_to_all | solution.py:385
  39.1 0.7 %shard_map.92 = f32[32,512]{1,0:T(8,128)} custom-call(f32[32,512]{1,0:T(8,128)S(1)} %get-tuple-element.108.runoff_ref, f32[40,512]{1,0:T(8,128)S(1)} %get-tuple-element.109.told_ref, f32[32,512]{1,0:T(8,128)S(1)} %select_add_fusion.arrive_ref), custom_call_target="tpu_custom_call" | custom-call | tf_op jit(solution)/shard_map/pallas_call | solution.py:532
  (11 shorter events, 0.1 us)
Async XLA Ops:
  8.9 3.4 %collective-permute-start = (f32[40,512]{1,0:T(8,128)S(1)}, f32[40,512]{1,0:T(8,128)S(1)}, u32[]{:S(2)}, u32[]{:S(2)}) collective-permute-start(f32[40,512]{1,0:T(8,128)S(1)} %param.1), channel_id=1, source_target_pairs={{0,16},{1,17},{2,18},{3,19},{4,20},{5,21},{6,22},{7,23},{8,24},{9,... | collective-permute-start | bytes 245768 | tf_op jit(solution)/shard_map/cond/branch_1_fun/ppermute | solution.py:451
  12.3 14.4 %collective-permute-start.4 = (f32[32,512]{1,0:T(8,128)S(1)}, f32[32,512]{1,0:T(8,128)S(1)}, u32[]{:S(2)}, u32[]{:S(2)}) collective-permute-start(f32[32,512]{1,0:T(8,128)S(1)} %get-tuple-element.128), channel_id=1, source_target_pairs={{0,24},{1,25},{2,26},{3,27},{4,28},{5,29},{6,30},{7,31}} | collective-permute-start | bytes 196616 | tf_op jit(solution)/shard_map/ppermute | solution.py:451
  13.6 10.8 %collective-permute-start.1 = (f32[104,512]{1,0:T(8,128)S(1)}, f32[104,512]{1,0:T(8,128)S(1)}, u32[]{:S(2)}, u32[]{:S(2)}) collective-permute-start(f32[104,512]{1,0:T(8,128)S(1)} %param.7), channel_id=1, source_target_pairs={{0,8},{1,9},{2,10},{3,11},{4,12},{5,13},{6,14},{7,15},{8,0},{9,1},... | collective-permute-start | bytes 638984 | tf_op jit(solution)/shard_map/cond/branch_1_fun/ppermute | solution.py:451

commit v4 on v3

--- a/solution.py
+++ b/solution.py
@@ -189,7 +189,6 @@
     gates = 4 * units
     per_block = units // channels
     capacity = 2 * reaches // basins
-    sums[...] = jnp.zeros_like(sums)
     for day in range(per_block):
         weights[day, units:, :] = jnp.zeros((units, gates), BF16)
     for load in loads[:-1]:
@@ -201,13 +200,12 @@
     recur = (jnp.transpose(w_recur_ref[...].astype(F32)) * (0.5 * scale)).astype(BF16)
     inputs = (w_input_ref[...].astype(F32) * scale).astype(BF16)
     bias = gate_bias_ref[...] * scale
-    readout = 0.5 * w_runoff_ref[...]
+    readout = as_column(0.5 * w_runoff_ref[...])
     for day in range(per_block):
         weights[day, :units, :] = recur
         weights[day, units + day * channels : units + (day + 1) * channels, :] = inputs
     chunk = min(CHUNK, reaches)
     chunks = reaches // chunk
-    lane = lax.broadcasted_iota(jnp.int32, (chunk, units), 1)
 
     info = known(drain_basin_ref[...], drain_reach_ref[...], travel_ref[...], weight_ref[...])
     told_ref[days:, :] = info
@@ -220,10 +218,12 @@
         blank_ref[...] = jnp.zeros_like(blank_ref)
     loads[-1].wait()
 
-    def block_of_days(block, state):
-        rows = pl.ds(pl.multiple_of(block * units, units), units)
+    state = [
+        (jnp.zeros((chunk, units), BF16), jnp.zeros((chunk, units), F32)) for _ in range(chunks)
+    ]
+    for block in range(days // per_block):
+        rows = slice(block * units, (block + 1) * units)
         forced = jnp.transpose(forcings_ref[rows, :].astype(F32)).astype(BF16)
-        state = list(state)
         for day in range(per_block):
             for part in range(chunks):
                 hidden, memory = state[part]
@@ -240,16 +240,13 @@
                 memory = 0.5 * ((forget * memory + memory) + (ingate * candidate + candidate))
                 squashed = jnp.tanh(memory)
                 hidden = (outgate * squashed + squashed).astype(BF16)
-                drained = jnp.sum(hidden.astype(F32) * readout, axis=1, keepdims=True)
-                sums[span, :] = jnp.where(lane == block * per_block + day, drained, sums[span, :])
+                drained = jnp.sum(
+                    jnp.transpose(hidden).astype(F32) * readout, axis=0, keepdims=True
+                )
+                now = block * per_block + day
+                sums[now : now + 1, span] = drained
                 state[part] = (hidden, memory)
-        return tuple(state)
-
-    state = tuple(
-        (jnp.zeros((chunk, units), BF16), jnp.zeros((chunk, units), F32)) for _ in range(chunks)
-    )
-    lax.fori_loop(0, days // per_block, block_of_days, state, unroll=True)
-    pre = jnp.transpose(sums[...])[:days]
+    pre = sums[...]
     runoff = jnp.maximum(pre, 0.0) + jnp.log1p(jnp.exp(-jnp.abs(pre)))
     runoff_ref[...] = runoff
     routed = route(runoff, coefficients_of(info))
@@ -433,7 +430,7 @@
         scratch_shapes=[pltpu.VMEM(array.shape, array.dtype) for array in operands]
         + [
             pltpu.VMEM((units // channels, 2 * units, 4 * units), BF16),
-            pltpu.VMEM((reaches, units), F32),
+            pltpu.VMEM((days, reaches), F32),
             pltpu.SemaphoreType.DMA((len(operands),)),
         ],
     )(*operands)
@@ -482,7 +479,7 @@
         absent,
     )
     arrive, passed, between = lax.optimization_barrier((arrive, passed, between))
-    passed = moved(passed, [(0, 3)] if groups > 3 else [])
+    passed = moved(passed, [(place, place ^ 3) for place in range(groups)])
     between = lax.cond(
         group > 1, lambda told: moved(told, neighbours), lambda told: told, between
     )

time: 40 us -> 39.4 us (0.985)
  waiting for transfers between devices: 5.68 us -> 5.1 us
    ppermute x3, waiting for transfers between devices: 5.68 us -> 5.1 us  [moved(): return lax.ppermute(block, ('order', 'basin'), pairs)]
where the time goes in v4:
time: 39.4 us; the launch traced here: 39.2 us
  blocking collectives  11.6 us (29%)
  starting transfers between devices  11.3 us (29%)
  Pallas kernels  11 us (28%)
  waiting for transfers between devices  5.1 us (13%)
    all_to_all x1, blocking collectives, swap(): lax.all_to_all(outgoing, 'basin', split_axis=0, concat_axis=0, tiled=True)  11.6 us
    ppermute x3, starting transfers between devices, moved(): return lax.ppermute(block, ('order', 'basin'), pairs)  11.3 us
    pallas_call x1, Pallas kernels, per_device(): call(functools.partial(first_body, days=days, basins=basins), [series(),...  8.79 us
    ppermute x3, waiting for transfers between devices, moved(): return lax.ppermute(block, ('order', 'basin'), pairs)  5.1 us
    pallas_call x1, Pallas kernels, per_device(): call(prepare_body, [ready_shape, paths_shape], 24)(*known[:2])  0.8 us
  transfers between devices with their start and end apart: 3, of which 3 were waited for; matrix products, arithmetic and copies ran while one was open for 0% of the time, Pallas kernels for 2%

profile of v4, /device:TPU:5, one launch (start us, length us, event | category | flops | bytes accessed | tf_op | source)
XLA Modules:
  0.0 39.2 jit_solution(14147753609155417986)
XLA Ops:
  0.0 8.8 %shard_map.91 = (f32[32,512]{1,0:T(8,128)S(1)}, f32[40,512]{1,0:T(8,128)S(1)}, f32[8,8,512]{2,1,0:T(8,128)S(1)}, f32[104,512]{1,0:T(8,128)S(1)}, f32[40,512]{1,0...) custom-call(bf16[512,512]{1,0:T(8,128)(2,1)} %bitcast.8, ...), custom_call_target="tpu_custom_call" | custom-call | tf_op jit(solution)/shard_map/pallas_call | solution.py:412
  8.8 3.4 %conditional.9 = (f32[40,512]{1,0:T(8,128)S(1)}) conditional(s32[]{:T(128)} %convert_element_type.30, f32[40,512]{1,0:T(8,128)S(1)} %get-tuple-element.115, f32[40,512]{1,0:T(8,128)S(1)} %get-tuple-element.109.told_ref), branch_computations={%region_0.1_spmd, %region_1.2_spmd} | conditional | bytes 491568 | solution.py:456
  8.8 0.1 collective-permute-start
  8.9 3.3 %collective-permute-done = f32[40,512]{1,0:T(8,128)S(1)} collective-permute-done((f32[40,512]{1,0:T(8,128)S(1)}, f32[40,512]{1,0:T(8,128)S(1)}, u32[]{:S(2)}, u32[]{:S(2)}) %collective-permute-start) | collective-permute-done | bytes 81952 | tf_op jit(solution)/shard_map/cond/branch_1_fun/ppermute | solution.py:448
  12.2 11.2 %collective-permute-start.4 = (f32[32,512]{1,0:T(8,128)S(1)}, f32[32,512]{1,0:T(8,128)S(1)}, u32[]{:S(2)}, u32[]{:S(2)}) collective-permute-start(f32[32,512]{1,0:T(8,128)S(1)} %get-tuple-element.128), channel_id=1, source_target_pairs={{0,24},{1,25},{2,26},{3,27},{4,28},{5,29},{6,30},{7,31},{8,16},{9,... | collective-permute-start | bytes 196616 | tf_op jit(solution)/shard_map/ppermute | solution.py:448
  23.4 1.5 %conditional.12 = (f32[104,512]{1,0:T(8,128)S(1)}) conditional(s32[]{:T(128)} %convert_element_type.32, f32[104,512]{1,0:T(8,128)S(1)} %get-tuple-element.144, f32[104,512]{1,0:T(8,128)S(1)} %get-tuple-element.144), branch_computations={%region_6.7_spmd, %region_7.8_spmd} | conditional | bytes 1278000 | solution.py:483
  23.4 0.0 collective-permute-start.1
  23.4 1.5 %collective-permute-done.1 = f32[104,512]{1,0:T(8,128)S(1)} collective-permute-done((f32[104,512]{1,0:T(8,128)S(1)}, f32[104,512]{1,0:T(8,128)S(1)}, u32[]{:S(2)}, u32[]{:S(2)}) %collective-permute-start.1) | collective-permute-done | bytes 213024 | tf_op jit(solution)/shard_map/cond/branch_1_fun/ppermute | solution.py:448
  24.9 0.8 %conditional.13 = ((f32[8,32,512]{2,1,0:T(8,128)S(1)}, f32[48,512]{1,0:T(8,128)S(1)})) conditional(s32[]{:T(128)} %convert_element_type.31, (f32[8,32,512]{2,1,0:T(8,128)S(1)}, f32[48,512]{1,0:T(8,128)S(1)}) %tuple.69, (f32[104,512]{1,0:T(8,128)S(1)}, f32[40,512]{1,0:T(8,128)S(1)}) %tuple.70), branch_computations={%region_8.9_spmd, %region_9.10_spmd} | conditional | bytes 8 | solution.py:486
  24.9 0.8 %branch_1_fun.9 = (f32[8,32,512]{2,1,0:T(8,128)S(1)}, f32[48,512]{1,0:T(8,128)S(1)}) custom-call(f32[104,512]{1,0:T(8,128)S(1)} %get-tuple-element.71.between_ref, f32[40,512]{1,0:T(8,128)S(1)} %get-tuple-element.72.above_ref), custom_call_target="tpu_custom_call" | custom-call | tf_op jit(solution)/shard_map/cond/branch_1_fun/pallas_call | solution.py:488
  25.8 0.4 collective-permute-done.4
  26.2 12.3 %conditional.16 = (f32[32,512]{1,0:T(8,128)S(1)}) conditional(s32[]{:T(128)} %convert_element_type.34, f32[32,512]{1,0:T(8,128)S(1)} %get-tuple-element.149, (f32[32,512]{1,0:T(8,128)S(1)}, f32[8,32,512]{2,1,0:T(8,128)S(1)}, f32[48,512]{1,0:T(8,128)S(1)}) %tuple.75), branch_computations={%region_14.15_spmd, %region_15.16_spmd} | conditional | bytes 1048584 | solution.py:513
  26.2 0.7 %branch_1_fun.12 = f32[8,32,512]{2,1,0:T(8,128)S(1)} custom-call(f32[32,512]{1,0:T(8,128)S(1)} %get-tuple-element.78.passed_ref, f32[8,32,512]{2,1,0:T(8,128)S(1)} %get-tuple-element.79.ready_ref, f32[48,512]{1,0:T(8,128)S(1)} %get-tuple-element.80.paths_ref), custom_call_target="tpu_custom_call" | custom-call | tf_op jit(solution)/shard_map/cond/branch_1_fun/pallas_call | solution.py:516
  26.9 11.6 %all_to_all.19.received_ref = f32[8,32,512]{2,1,0:T(8,128)S(1)} all-to-all(f32[8,32,512]{2,1,0:T(8,128)S(1)} %branch_1_fun.12), channel_id=1, replica_groups=mesh['order'=4,'basin'=8] {'basin'}, dimensions={0} | all-to-all | bytes 1048576 | tf_op jit(solution)/shard_map/cond/branch_1_fun/all_to_all | solution.py:382
  38.5 0.7 %shard_map.92 = f32[32,512]{1,0:T(8,128)} custom-call(f32[32,512]{1,0:T(8,128)S(1)} %get-tuple-element.108.runoff_ref, f32[40,512]{1,0:T(8,128)S(1)} %get-tuple-element.109.told_ref, f32[32,512]{1,0:T(8,128)S(1)} %select_add_fusion.arrive_ref), custom_call_target="tpu_custom_call" | custom-call | tf_op jit(solution)/shard_map/pallas_call | solution.py:529
  (11 shorter events, 0.1 us)
Async XLA Ops:
  8.8 3.4 %collective-permute-start = (f32[40,512]{1,0:T(8,128)S(1)}, f32[40,512]{1,0:T(8,128)S(1)}, u32[]{:S(2)}, u32[]{:S(2)}) collective-permute-start(f32[40,512]{1,0:T(8,128)S(1)} %param.1), channel_id=1, source_target_pairs={{0,16},{1,17},{2,18},{3,19},{4,20},{5,21},{6,22},{7,23},{8,24},{9,... | collective-permute-start | bytes 245768 | tf_op jit(solution)/shard_map/cond/branch_1_fun/ppermute | solution.py:448
  12.2 14.0 %collective-permute-start.4 = (f32[32,512]{1,0:T(8,128)S(1)}, f32[32,512]{1,0:T(8,128)S(1)}, u32[]{:S(2)}, u32[]{:S(2)}) collective-permute-start(f32[32,512]{1,0:T(8,128)S(1)} %get-tuple-element.128), channel_id=1, source_target_pairs={{0,24},{1,25},{2,26},{3,27},{4,28},{5,29},{6,30},{7,31},{8,16},{9,... | collective-permute-start | bytes 196616 | tf_op jit(solution)/shard_map/ppermute | solution.py:448
  23.4 1.5 %collective-permute-start.1 = (f32[104,512]{1,0:T(8,128)S(1)}, f32[104,512]{1,0:T(8,128)S(1)}, u32[]{:S(2)}, u32[]{:S(2)}) collective-permute-start(f32[104,512]{1,0:T(8,128)S(1)} %param.7), channel_id=1, source_target_pairs={{0,8},{1,9},{2,10},{3,11},{4,12},{5,13},{6,14},{7,15},{8,0},{9,1},... | collective-permute-start | bytes 638984 | tf_op jit(solution)/shard_map/cond/branch_1_fun/ppermute | solution.py:448

commit v5 on v4

--- a/solution.py
+++ b/solution.py
@@ -187,10 +187,12 @@
     channels = forcings_ref.shape[0] // days
     units = w_recur_ref.shape[1]
     gates = 4 * units
-    per_block = units // channels
+    per_block = units // channels - 1
     capacity = 2 * reaches // basins
     for day in range(per_block):
         weights[day, units:, :] = jnp.zeros((units, gates), BF16)
+    for blank_ref in (between_ref, above_ref, ready_ref, paths_ref, missing_ref, absent_ref):
+        blank_ref[...] = jnp.zeros_like(blank_ref)
     for load in loads[:-1]:
         load.wait()
 
@@ -199,11 +201,14 @@
     scale = jnp.where(is_candidate, 1.0, 0.5)
     recur = (jnp.transpose(w_recur_ref[...].astype(F32)) * (0.5 * scale)).astype(BF16)
     inputs = (w_input_ref[...].astype(F32) * scale).astype(BF16)
-    bias = gate_bias_ref[...] * scale
+    thirds = [third.astype(F32) for third in in_thirds(gate_bias_ref[...] * scale)]
+    blank = jnp.zeros((channels - len(thirds), gates), F32)
+    biases = jnp.concatenate([*thirds, blank], axis=0).astype(BF16)
     readout = as_column(0.5 * w_runoff_ref[...])
     for day in range(per_block):
         weights[day, :units, :] = recur
         weights[day, units + day * channels : units + (day + 1) * channels, :] = inputs
+        weights[day, units + per_block * channels :, :] = biases
     chunk = min(CHUNK, reaches)
     chunks = reaches // chunk
 
@@ -214,21 +219,23 @@
     send_table, targets = slot_tables(drain_basin_ref[...], drain_reach_ref[...], basins, capacity)
     send_table_ref[...] = send_table
     targets_ref[...] = targets
-    for blank_ref in (between_ref, above_ref, ready_ref, paths_ref, missing_ref, absent_ref):
-        blank_ref[...] = jnp.zeros_like(blank_ref)
     loads[-1].wait()
 
     state = [
         (jnp.zeros((chunk, units), BF16), jnp.zeros((chunk, units), F32)) for _ in range(chunks)
     ]
-    for block in range(days // per_block):
-        rows = slice(block * units, (block + 1) * units)
-        forced = jnp.transpose(forcings_ref[rows, :].astype(F32)).astype(BF16)
-        for day in range(per_block):
+    for first in range(0, days, per_block):
+        count = min(per_block, days - first)
+        forced = [forcings_ref[first * channels : (first + count) * channels, :].astype(F32)]
+        if count < per_block:
+            forced.append(jnp.zeros(((per_block - count) * channels, reaches), F32))
+        forced.append(jnp.ones((channels, reaches), F32))
+        forced = jnp.transpose(jnp.concatenate(forced, axis=0)).astype(BF16)
+        for day in range(count):
             for part in range(chunks):
                 hidden, memory = state[part]
                 span = slice(part * chunk, (part + 1) * chunk)
-                gate_sums = bias + jnp.dot(
+                gate_sums = jnp.dot(
                     jnp.concatenate([hidden, forced[span]], axis=1),
                     weights[day],
                     preferred_element_type=F32,
@@ -243,8 +250,7 @@
                 drained = jnp.sum(
                     jnp.transpose(hidden).astype(F32) * readout, axis=0, keepdims=True
                 )
-                now = block * per_block + day
-                sums[now : now + 1, span] = drained
+                sums[first + day : first + day + 1, span] = drained
                 state[part] = (hidden, memory)
     pre = sums[...]
     runoff = jnp.maximum(pre, 0.0) + jnp.log1p(jnp.exp(-jnp.abs(pre)))
@@ -429,7 +435,7 @@
         in_specs=[pl.BlockSpec(memory_space=pltpu.HBM) for _ in operands],
         scratch_shapes=[pltpu.VMEM(array.shape, array.dtype) for array in operands]
         + [
-            pltpu.VMEM((units // channels, 2 * units, 4 * units), BF16),
+            pltpu.VMEM((units // channels - 1, 2 * units, 4 * units), BF16),
             pltpu.VMEM((days, reaches), F32),
             pltpu.SemaphoreType.DMA((len(operands),)),
         ],

time: 39.4 us -> 38.8 us (0.985)
  Pallas kernels: 11 us -> 10.5 us
    pallas_call x1, Pallas kernels: 8.79 us -> 8.21 us  [per_device(): call(functools.partial(first_body, days=days, basins=basins), [series(),...]
where the time goes in v5:
time: 38.8 us; the launch traced here: 38.7 us
  blocking collectives  11.6 us (30%)
  starting transfers between devices  11.3 us (29%)
  Pallas kernels  10.5 us (27%)
  waiting for transfers between devices  5.11 us (13%)
    all_to_all x1, blocking collectives, swap(): lax.all_to_all(outgoing, 'basin', split_axis=0, concat_axis=0, tiled=True)  11.6 us
    ppermute x3, starting transfers between devices, moved(): return lax.ppermute(block, ('order', 'basin'), pairs)  11.3 us
    pallas_call x1, Pallas kernels, per_device(): call(functools.partial(first_body, days=days, basins=basins), [series(),...  8.21 us
    ppermute x3, waiting for transfers between devices, moved(): return lax.ppermute(block, ('order', 'basin'), pairs)  5.11 us
    pallas_call x1, Pallas kernels, per_device(): call(prepare_body, [ready_shape, paths_shape], 24)(*known[:2])  0.8 us
  transfers between devices with their start and end apart: 3, of which 3 were waited for; matrix products, arithmetic and copies ran while one was open for 0% of the time, Pallas kernels for 2%

profile of v5, /device:TPU:5, one launch (start us, length us, event | category | flops | bytes accessed | tf_op | source)
XLA Modules:
  0.0 38.7 jit_solution(6042651714351787541)
XLA Ops:
  0.0 8.2 %shard_map.91 = (f32[32,512]{1,0:T(8,128)S(1)}, f32[40,512]{1,0:T(8,128)S(1)}, f32[8,8,512]{2,1,0:T(8,128)S(1)}, f32[104,512]{1,0:T(8,128)S(1)}, f32[40,512]{1,0...) custom-call(bf16[512,512]{1,0:T(8,128)(2,1)} %bitcast.8, ...), custom_call_target="tpu_custom_call" | custom-call | tf_op jit(solution)/shard_map/pallas_call | solution.py:418
  8.2 3.4 %conditional.9 = (f32[40,512]{1,0:T(8,128)S(1)}) conditional(s32[]{:T(128)} %convert_element_type.30, f32[40,512]{1,0:T(8,128)S(1)} %get-tuple-element.115, f32[40,512]{1,0:T(8,128)S(1)} %get-tuple-element.109.told_ref), branch_computations={%region_0.1_spmd, %region_1.2_spmd} | conditional | bytes 491568 | solution.py:462
  8.2 0.1 collective-permute-start
  8.3 3.3 %collective-permute-done = f32[40,512]{1,0:T(8,128)S(1)} collective-permute-done((f32[40,512]{1,0:T(8,128)S(1)}, f32[40,512]{1,0:T(8,128)S(1)}, u32[]{:S(2)}, u32[]{:S(2)}) %collective-permute-start) | collective-permute-done | bytes 81952 | tf_op jit(solution)/shard_map/cond/branch_1_fun/ppermute | solution.py:454
  11.6 11.2 %collective-permute-start.4 = (f32[32,512]{1,0:T(8,128)S(1)}, f32[32,512]{1,0:T(8,128)S(1)}, u32[]{:S(2)}, u32[]{:S(2)}) collective-permute-start(f32[32,512]{1,0:T(8,128)S(1)} %get-tuple-element.128), channel_id=1, source_target_pairs={{0,24},{1,25},{2,26},{3,27},{4,28},{5,29},{6,30},{7,31},{8,16},{9,... | collective-permute-start | bytes 196616 | tf_op jit(solution)/shard_map/ppermute | solution.py:454
  22.8 1.5 %conditional.12 = (f32[104,512]{1,0:T(8,128)S(1)}) conditional(s32[]{:T(128)} %convert_element_type.32, f32[104,512]{1,0:T(8,128)S(1)} %get-tuple-element.144, f32[104,512]{1,0:T(8,128)S(1)} %get-tuple-element.144), branch_computations={%region_6.7_spmd, %region_7.8_spmd} | conditional | bytes 1278000 | solution.py:489
  22.8 0.0 collective-permute-start.1
  22.8 1.5 %collective-permute-done.1 = f32[104,512]{1,0:T(8,128)S(1)} collective-permute-done((f32[104,512]{1,0:T(8,128)S(1)}, f32[104,512]{1,0:T(8,128)S(1)}, u32[]{:S(2)}, u32[]{:S(2)}) %collective-permute-start.1) | collective-permute-done | bytes 213024 | tf_op jit(solution)/shard_map/cond/branch_1_fun/ppermute | solution.py:454
  24.3 0.8 %conditional.13 = ((f32[8,32,512]{2,1,0:T(8,128)S(1)}, f32[48,512]{1,0:T(8,128)S(1)})) conditional(s32[]{:T(128)} %convert_element_type.31, (f32[8,32,512]{2,1,0:T(8,128)S(1)}, f32[48,512]{1,0:T(8,128)S(1)}) %tuple.69, (f32[104,512]{1,0:T(8,128)S(1)}, f32[40,512]{1,0:T(8,128)S(1)}) %tuple.70), branch_computations={%region_8.9_spmd, %region_9.10_spmd} | conditional | bytes 8 | solution.py:492
  24.3 0.8 %branch_1_fun.9 = (f32[8,32,512]{2,1,0:T(8,128)S(1)}, f32[48,512]{1,0:T(8,128)S(1)}) custom-call(f32[104,512]{1,0:T(8,128)S(1)} %get-tuple-element.71.between_ref, f32[40,512]{1,0:T(8,128)S(1)} %get-tuple-element.72.above_ref), custom_call_target="tpu_custom_call" | custom-call | tf_op jit(solution)/shard_map/cond/branch_1_fun/pallas_call | solution.py:494
  25.2 0.4 collective-permute-done.4
  25.6 12.3 %conditional.16 = (f32[32,512]{1,0:T(8,128)S(1)}) conditional(s32[]{:T(128)} %convert_element_type.34, f32[32,512]{1,0:T(8,128)S(1)} %get-tuple-element.149, (f32[32,512]{1,0:T(8,128)S(1)}, f32[8,32,512]{2,1,0:T(8,128)S(1)}, f32[48,512]{1,0:T(8,128)S(1)}) %tuple.75), branch_computations={%region_14.15_spmd, %region_15.16_spmd} | conditional | bytes 1048584 | solution.py:519
  25.6 0.7 %branch_1_fun.12 = f32[8,32,512]{2,1,0:T(8,128)S(1)} custom-call(f32[32,512]{1,0:T(8,128)S(1)} %get-tuple-element.78.passed_ref, f32[8,32,512]{2,1,0:T(8,128)S(1)} %get-tuple-element.79.ready_ref, f32[48,512]{1,0:T(8,128)S(1)} %get-tuple-element.80.paths_ref), custom_call_target="tpu_custom_call" | custom-call | tf_op jit(solution)/shard_map/cond/branch_1_fun/pallas_call | solution.py:522
  26.3 11.6 %all_to_all.19.received_ref = f32[8,32,512]{2,1,0:T(8,128)S(1)} all-to-all(f32[8,32,512]{2,1,0:T(8,128)S(1)} %branch_1_fun.12), channel_id=1, replica_groups=mesh['order'=4,'basin'=8] {'basin'}, dimensions={0} | all-to-all | bytes 1048576 | tf_op jit(solution)/shard_map/cond/branch_1_fun/all_to_all | solution.py:388
  38.0 0.7 %shard_map.92 = f32[32,512]{1,0:T(8,128)} custom-call(f32[32,512]{1,0:T(8,128)S(1)} %get-tuple-element.108.runoff_ref, f32[40,512]{1,0:T(8,128)S(1)} %get-tuple-element.109.told_ref, f32[32,512]{1,0:T(8,128)S(1)} %select_add_fusion.arrive_ref), custom_call_target="tpu_custom_call" | custom-call | tf_op jit(solution)/shard_map/pallas_call | solution.py:535
  (11 shorter events, 0.1 us)
Async XLA Ops:
  8.2 3.4 %collective-permute-start = (f32[40,512]{1,0:T(8,128)S(1)}, f32[40,512]{1,0:T(8,128)S(1)}, u32[]{:S(2)}, u32[]{:S(2)}) collective-permute-start(f32[40,512]{1,0:T(8,128)S(1)} %param.1), channel_id=1, source_target_pairs={{0,16},{1,17},{2,18},{3,19},{4,20},{5,21},{6,22},{7,23},{8,24},{9,... | collective-permute-start | bytes 245768 | tf_op jit(solution)/shard_map/cond/branch_1_fun/ppermute | solution.py:454
  11.6 14.0 %collective-permute-start.4 = (f32[32,512]{1,0:T(8,128)S(1)}, f32[32,512]{1,0:T(8,128)S(1)}, u32[]{:S(2)}, u32[]{:S(2)}) collective-permute-start(f32[32,512]{1,0:T(8,128)S(1)} %get-tuple-element.128), channel_id=1, source_target_pairs={{0,24},{1,25},{2,26},{3,27},{4,28},{5,29},{6,30},{7,31},{8,16},{9,... | collective-permute-start | bytes 196616 | tf_op jit(solution)/shard_map/ppermute | solution.py:454
  22.8 1.5 %collective-permute-start.1 = (f32[104,512]{1,0:T(8,128)S(1)}, f32[104,512]{1,0:T(8,128)S(1)}, u32[]{:S(2)}, u32[]{:S(2)}) collective-permute-start(f32[104,512]{1,0:T(8,128)S(1)} %param.7), channel_id=1, source_target_pairs={{0,8},{1,9},{2,10},{3,11},{4,12},{5,13},{6,14},{7,15},{8,0},{9,1},... | collective-permute-start | bytes 638984 | tf_op jit(solution)/shard_map/cond/branch_1_fun/ppermute | solution.py:454

commit v6 on v5

--- a/solution.py
+++ b/solution.py
@@ -226,11 +226,11 @@
     ]
     for first in range(0, days, per_block):
         count = min(per_block, days - first)
-        forced = [forcings_ref[first * channels : (first + count) * channels, :].astype(F32)]
+        forced = [forcings_ref[first * channels : (first + count) * channels, :]]
         if count < per_block:
-            forced.append(jnp.zeros(((per_block - count) * channels, reaches), F32))
-        forced.append(jnp.ones((channels, reaches), F32))
-        forced = jnp.transpose(jnp.concatenate(forced, axis=0)).astype(BF16)
+            forced.append(jnp.zeros(((per_block - count) * channels, reaches), BF16))
+        forced.append(jnp.ones((channels, reaches), BF16))
+        forced = jnp.transpose(jnp.concatenate(forced, axis=0))
         for day in range(count):
             for part in range(chunks):
                 hidden, memory = state[part]

time: 38.8 us -> 38.8 us (level)
  no operation moved by 1% of the time
where the time goes in v6:
time: 38.8 us; the launch traced here: 38.6 us
  blocking collectives  11.6 us (30%)
  starting transfers between devices  11.3 us (29%)
  Pallas kernels  10.4 us (27%)
  waiting for transfers between devices  5.12 us (13%)
    all_to_all x1, blocking collectives, swap(): lax.all_to_all(outgoing, 'basin', split_axis=0, concat_axis=0, tiled=True)  11.6 us
    ppermute x3, starting transfers between devices, moved(): return lax.ppermute(block, ('order', 'basin'), pairs)  11.3 us
    pallas_call x1, Pallas kernels, per_device(): call(functools.partial(first_body, days=days, basins=basins), [series(),...  8.18 us
    ppermute x3, waiting for transfers between devices, moved(): return lax.ppermute(block, ('order', 'basin'), pairs)  5.12 us
    pallas_call x1, Pallas kernels, per_device(): call(prepare_body, [ready_shape, paths_shape], 24)(*known[:2])  0.79 us
  transfers between devices with their start and end apart: 3, of which 3 were waited for; matrix products, arithmetic and copies ran while one was open for 0% of the time, Pallas kernels for 2%

profile of v6, /device:TPU:5, one launch (start us, length us, event | category | flops | bytes accessed | tf_op | source)
XLA Modules:
  0.0 38.6 jit_solution(17850042915886516643)
XLA Ops:
  0.0 8.2 %shard_map.91 = (f32[32,512]{1,0:T(8,128)S(1)}, f32[40,512]{1,0:T(8,128)S(1)}, f32[8,8,512]{2,1,0:T(8,128)S(1)}, f32[104,512]{1,0:T(8,128)S(1)}, f32[40,512]{1,0...) custom-call(bf16[512,512]{1,0:T(8,128)(2,1)} %bitcast.8, ...), custom_call_target="tpu_custom_call" | custom-call | tf_op jit(solution)/shard_map/pallas_call | solution.py:418
  8.2 3.4 %conditional.9 = (f32[40,512]{1,0:T(8,128)S(1)}) conditional(s32[]{:T(128)} %convert_element_type.30, f32[40,512]{1,0:T(8,128)S(1)} %get-tuple-element.115, f32[40,512]{1,0:T(8,128)S(1)} %get-tuple-element.109.told_ref), branch_computations={%region_0.1_spmd, %region_1.2_spmd} | conditional | bytes 491568 | solution.py:462
  8.2 0.1 collective-permute-start
  8.3 3.3 %collective-permute-done = f32[40,512]{1,0:T(8,128)S(1)} collective-permute-done((f32[40,512]{1,0:T(8,128)S(1)}, f32[40,512]{1,0:T(8,128)S(1)}, u32[]{:S(2)}, u32[]{:S(2)}) %collective-permute-start) | collective-permute-done | bytes 81952 | tf_op jit(solution)/shard_map/cond/branch_1_fun/ppermute | solution.py:454
  11.6 11.2 %collective-permute-start.4 = (f32[32,512]{1,0:T(8,128)S(1)}, f32[32,512]{1,0:T(8,128)S(1)}, u32[]{:S(2)}, u32[]{:S(2)}) collective-permute-start(f32[32,512]{1,0:T(8,128)S(1)} %get-tuple-element.128), channel_id=1, source_target_pairs={{0,24},{1,25},{2,26},{3,27},{4,28},{5,29},{6,30},{7,31},{8,16},{9,... | collective-permute-start | bytes 196616 | tf_op jit(solution)/shard_map/ppermute | solution.py:454
  22.8 1.5 %conditional.12 = (f32[104,512]{1,0:T(8,128)S(1)}) conditional(s32[]{:T(128)} %convert_element_type.32, f32[104,512]{1,0:T(8,128)S(1)} %get-tuple-element.144, f32[104,512]{1,0:T(8,128)S(1)} %get-tuple-element.144), branch_computations={%region_6.7_spmd, %region_7.8_spmd} | conditional | bytes 1278000 | solution.py:489
  22.8 0.0 collective-permute-start.1
  22.8 1.5 %collective-permute-done.1 = f32[104,512]{1,0:T(8,128)S(1)} collective-permute-done((f32[104,512]{1,0:T(8,128)S(1)}, f32[104,512]{1,0:T(8,128)S(1)}, u32[]{:S(2)}, u32[]{:S(2)}) %collective-permute-start.1) | collective-permute-done | bytes 213024 | tf_op jit(solution)/shard_map/cond/branch_1_fun/ppermute | solution.py:454
  24.3 0.8 %conditional.13 = ((f32[8,32,512]{2,1,0:T(8,128)S(1)}, f32[48,512]{1,0:T(8,128)S(1)})) conditional(s32[]{:T(128)} %convert_element_type.31, (f32[8,32,512]{2,1,0:T(8,128)S(1)}, f32[48,512]{1,0:T(8,128)S(1)}) %tuple.69, (f32[104,512]{1,0:T(8,128)S(1)}, f32[40,512]{1,0:T(8,128)S(1)}) %tuple.70), branch_computations={%region_8.9_spmd, %region_9.10_spmd} | conditional | bytes 8 | solution.py:492
  24.3 0.8 %branch_1_fun.9 = (f32[8,32,512]{2,1,0:T(8,128)S(1)}, f32[48,512]{1,0:T(8,128)S(1)}) custom-call(f32[104,512]{1,0:T(8,128)S(1)} %get-tuple-element.71.between_ref, f32[40,512]{1,0:T(8,128)S(1)} %get-tuple-element.72.above_ref), custom_call_target="tpu_custom_call" | custom-call | tf_op jit(solution)/shard_map/cond/branch_1_fun/pallas_call | solution.py:494
  25.2 0.4 collective-permute-done.4
  25.6 12.3 %conditional.16 = (f32[32,512]{1,0:T(8,128)S(1)}) conditional(s32[]{:T(128)} %convert_element_type.34, f32[32,512]{1,0:T(8,128)S(1)} %get-tuple-element.149, (f32[32,512]{1,0:T(8,128)S(1)}, f32[8,32,512]{2,1,0:T(8,128)S(1)}, f32[48,512]{1,0:T(8,128)S(1)}) %tuple.75), branch_computations={%region_14.15_spmd, %region_15.16_spmd} | conditional | bytes 1048584 | solution.py:519
  25.6 0.7 %branch_1_fun.12 = f32[8,32,512]{2,1,0:T(8,128)S(1)} custom-call(f32[32,512]{1,0:T(8,128)S(1)} %get-tuple-element.78.passed_ref, f32[8,32,512]{2,1,0:T(8,128)S(1)} %get-tuple-element.79.ready_ref, f32[48,512]{1,0:T(8,128)S(1)} %get-tuple-element.80.paths_ref), custom_call_target="tpu_custom_call" | custom-call | tf_op jit(solution)/shard_map/cond/branch_1_fun/pallas_call | solution.py:522
  26.3 11.6 %all_to_all.19.received_ref = f32[8,32,512]{2,1,0:T(8,128)S(1)} all-to-all(f32[8,32,512]{2,1,0:T(8,128)S(1)} %branch_1_fun.12), channel_id=1, replica_groups=mesh['order'=4,'basin'=8] {'basin'}, dimensions={0} | all-to-all | bytes 1048576 | tf_op jit(solution)/shard_map/cond/branch_1_fun/all_to_all | solution.py:388
  37.9 0.7 %shard_map.92 = f32[32,512]{1,0:T(8,128)} custom-call(f32[32,512]{1,0:T(8,128)S(1)} %get-tuple-element.108.runoff_ref, f32[40,512]{1,0:T(8,128)S(1)} %get-tuple-element.109.told_ref, f32[32,512]{1,0:T(8,128)S(1)} %select_add_fusion.arrive_ref), custom_call_target="tpu_custom_call" | custom-call | tf_op jit(solution)/shard_map/pallas_call | solution.py:535
  (11 shorter events, 0.1 us)
Async XLA Ops:
  8.2 3.4 %collective-permute-start = (f32[40,512]{1,0:T(8,128)S(1)}, f32[40,512]{1,0:T(8,128)S(1)}, u32[]{:S(2)}, u32[]{:S(2)}) collective-permute-start(f32[40,512]{1,0:T(8,128)S(1)} %param.1), channel_id=1, source_target_pairs={{0,16},{1,17},{2,18},{3,19},{4,20},{5,21},{6,22},{7,23},{8,24},{9,... | collective-permute-start | bytes 245768 | tf_op jit(solution)/shard_map/cond/branch_1_fun/ppermute | solution.py:454
  11.6 14.0 %collective-permute-start.4 = (f32[32,512]{1,0:T(8,128)S(1)}, f32[32,512]{1,0:T(8,128)S(1)}, u32[]{:S(2)}, u32[]{:S(2)}) collective-permute-start(f32[32,512]{1,0:T(8,128)S(1)} %get-tuple-element.128), channel_id=1, source_target_pairs={{0,24},{1,25},{2,26},{3,27},{4,28},{5,29},{6,30},{7,31},{8,16},{9,... | collective-permute-start | bytes 196616 | tf_op jit(solution)/shard_map/ppermute | solution.py:454
  22.8 1.5 %collective-permute-start.1 = (f32[104,512]{1,0:T(8,128)S(1)}, f32[104,512]{1,0:T(8,128)S(1)}, u32[]{:S(2)}, u32[]{:S(2)}) collective-permute-start(f32[104,512]{1,0:T(8,128)S(1)} %param.7), channel_id=1, source_target_pairs={{0,8},{1,9},{2,10},{3,11},{4,12},{5,13},{6,14},{7,15},{8,0},{9,1},... | collective-permute-start | bytes 638984 | tf_op jit(solution)/shard_map/cond/branch_1_fun/ppermute | solution.py:454

commit v7 on v6

--- a/solution.py
+++ b/solution.py
@@ -144,6 +144,7 @@
     above_ref,
     ready_ref,
     paths_ref,
+    pick_ref,
     missing_ref,
     absent_ref,
     send_table_ref,
@@ -191,7 +192,8 @@
     capacity = 2 * reaches // basins
     for day in range(per_block):
         weights[day, units:, :] = jnp.zeros((units, gates), BF16)
-    for blank_ref in (between_ref, above_ref, ready_ref, paths_ref, missing_ref, absent_ref):
+    blanks = (between_ref, above_ref, ready_ref, paths_ref, pick_ref, missing_ref, absent_ref)
+    for blank_ref in blanks:
         blank_ref[...] = jnp.zeros_like(blank_ref)
     for load in loads[:-1]:
         load.wait()
@@ -292,15 +294,15 @@
 def bundle_body(told_ref, tables_ref, bundle_ref):
     rows = told_ref.shape[0]
     bundle_ref[:rows, :] = told_ref[...]
-    for basin in range(tables_ref.shape[0]):
-        first = rows + basin * INFO_ROWS
-        bundle_ref[first : first + INFO_ROWS, :] = tables_ref[basin]
+    bundle_ref[rows:, :] = jnp.concatenate(
+        [tables_ref[basin, :KNOWN, :] for basin in range(tables_ref.shape[0])], axis=0
+    )
 
 
 def info_table(tables):
     pieces = []
-    for first in range(0, tables.shape[0], INFO_ROWS):
-        info = tables[first : first + INFO_ROWS]
+    for first in range(0, tables.shape[0], KNOWN):
+        info = tables[first : first + KNOWN]
         reach = info[1:2].astype(jnp.int32)
         rows = [info[0:1], (reach // 16).astype(F32), (reach % 16).astype(F32)]
         for row in range(2, KNOWN):
@@ -310,10 +312,15 @@
     return jnp.concatenate(pieces, axis=0)
 
 
-def looked_up(table, from_basin, from_reach):
+def pick_body(above_ref, pick_ref):
+    reaches = pick_ref.shape[1]
+    days = above_ref.shape[0] - INFO_ROWS
+    sublanes = lax.broadcasted_iota(jnp.int32, (reaches, reaches), 0).astype(F32)
+    pick_ref[...] = jnp.where(sublanes == above_ref[days + 1 : days + 2, :], 1.0, 0.0).astype(BF16)
+
+
+def looked_up(table, from_basin, pick):
     reaches = table.shape[1]
-    sublanes = lax.broadcasted_iota(jnp.int32, (reaches, reaches), 0).astype(F32)
-    pick = jnp.where(sublanes == from_reach, 1.0, 0.0).astype(BF16)
     picked = jnp.dot(table, pick, preferred_element_type=F32)
     found = jnp.zeros((TABLE_ROWS, reaches), F32)
     for basin in range(table.shape[0] // TABLE_ROWS):
@@ -340,11 +347,11 @@
     ]
 
 
-def prepare_body(between_ref, above_ref, ready_ref, paths_ref):
+def prepare_body(between_ref, above_ref, pick_ref, ready_ref, paths_ref):
     basins, days, reaches = ready_ref.shape
     rows = days + INFO_ROWS
     to_basin, to_reach, coefficients = looked_up(
-        info_table(between_ref[rows:, :]), above_ref[days : days + 1, :], above_ref[days + 1 : days + 2, :]
+        info_table(between_ref[rows:, :]), above_ref[days : days + 1, :], pick_ref[...]
     )
     paths_ref[:rows, :] = above_ref[...]
     blank = jnp.zeros((INFO_ROWS - KNOWN, reaches), F32)
@@ -409,13 +416,14 @@
         row(drain_reach),
     )
     told_shape = jax.ShapeDtypeStruct((days + INFO_ROWS, reaches), F32)
-    bundle_shape = jax.ShapeDtypeStruct((days + (1 + basins) * INFO_ROWS, reaches), F32)
+    bundle_shape = jax.ShapeDtypeStruct((days + INFO_ROWS + basins * KNOWN, reaches), F32)
     ready_shape = jax.ShapeDtypeStruct((basins, days, reaches), F32)
+    pick_shape = jax.ShapeDtypeStruct((reaches, reaches), BF16)
     paths_shape = jax.ShapeDtypeStruct((days + 2 * INFO_ROWS, reaches), F32)
     payload_shape = jax.ShapeDtypeStruct(
         (basins, days + ID_ROWS, capacity) if split else (days + ID_ROWS, slots), F32
     )
-    runoff, told, spread, between, above, ready, paths, *late = call(
+    runoff, told, spread, between, above, ready, paths, pick, *late = call(
         functools.partial(first_body, days=days, basins=basins),
         [
             series(),
@@ -425,6 +433,7 @@
             told_shape,
             ready_shape,
             paths_shape,
+            pick_shape,
             series(),
             series(),
             jax.ShapeDtypeStruct((reaches, slots), BF16),
@@ -462,7 +471,14 @@
     above = lax.cond(
         group % 2 == 1, lambda told, blank: moved(told, two_down), lambda _, blank: blank, told, above
     )
-    spread, above = lax.optimization_barrier((spread, above))
+    pick = lax.cond(
+        (group % 2 == 1) & (group > 1),
+        lambda above, _: call(pick_body, pick_shape)(above),
+        lambda above, blank: blank,
+        above,
+        pick,
+    )
+    spread, above, pick = lax.optimization_barrier((spread, above, pick))
     between = lax.cond(
         (group % 2 == 0) & (group > 1),
         lambda spread, told, _: call(bundle_body, bundle_shape)(told, swap(spread)),
@@ -491,10 +507,11 @@
     )
     ready, paths = lax.cond(
         (group % 2 == 1) & (group > 1),
-        lambda *known: tuple(call(prepare_body, [ready_shape, paths_shape], 24)(*known[:2])),
-        lambda between, above, ready, paths: (ready, paths),
+        lambda *known: tuple(call(prepare_body, [ready_shape, paths_shape], 24)(*known[:3])),
+        lambda between, above, pick, ready, paths: (ready, paths),
         between,
         above,
+        pick,
         ready,
         paths,
     )

time: 38.8 us -> 38.8 us (level)
    pallas_call x1 -> x2, Pallas kernels: 0.79 us -> 0.84 us  [the longest x1 0.73 us: per_device(): call(prepare_body, [ready_shape, paths_shape], 24)(*known[:3])]
where the time goes in v7:
time: 38.8 us; the launch traced here: 38.6 us
  blocking collectives  11.6 us (30%)
  starting transfers between devices  11.2 us (29%)
  Pallas kernels  10.5 us (27%)
  waiting for transfers between devices  5.17 us (13%)
    all_to_all x1, blocking collectives, swap(): lax.all_to_all(outgoing, 'basin', split_axis=0, concat_axis=0, tiled=True)  11.6 us
    ppermute x3, starting transfers between devices, moved(): return lax.ppermute(block, ('order', 'basin'), pairs)  11.2 us
    pallas_call x1, Pallas kernels, per_device(): call(functools.partial(first_body, days=days, basins=basins), [series(),...  8.19 us
    ppermute x3, waiting for transfers between devices, moved(): return lax.ppermute(block, ('order', 'basin'), pairs)  5.17 us
  transfers between devices with their start and end apart: 3, of which 3 were waited for; matrix products, arithmetic and copies ran while one was open for 0% of the time, Pallas kernels for 2%

profile of v7, /device:TPU:5, one launch (start us, length us, event | category | flops | bytes accessed | tf_op | source)
XLA Modules:
  0.0 38.6 jit_solution(15909638239865002191)
XLA Ops:
  0.0 8.2 %shard_map.91 = (f32[32,512]{1,0:T(8,128)S(1)}, f32[40,512]{1,0:T(8,128)S(1)}, f32[8,8,512]{2,1,0:T(8,128)S(1)}, f32[80,512]{1,0:T(8,128)S(1)}, f32[40,512]{1,0:...) custom-call(bf16[512,512]{1,0:T(8,128)(2,1)} %bitcast.8, ...), custom_call_target="tpu_custom_call" | custom-call | tf_op jit(solution)/shard_map/pallas_call | solution.py:426
  8.2 3.4 %conditional.10 = (f32[40,512]{1,0:T(8,128)S(1)}) conditional(s32[]{:T(128)} %convert_element_type.31, f32[40,512]{1,0:T(8,128)S(1)} %get-tuple-element.125, f32[40,512]{1,0:T(8,128)S(1)} %get-tuple-element.119.told_ref), branch_computations={%region_0.1_spmd, %region_1.2_spmd} | conditional | bytes 491568 | solution.py:471
  8.2 0.1 collective-permute-start
  8.3 3.3 %collective-permute-done = f32[40,512]{1,0:T(8,128)S(1)} collective-permute-done((f32[40,512]{1,0:T(8,128)S(1)}, f32[40,512]{1,0:T(8,128)S(1)}, u32[]{:S(2)}, u32[]{:S(2)}) %collective-permute-start) | collective-permute-done | bytes 81952 | tf_op jit(solution)/shard_map/cond/branch_1_fun/ppermute | solution.py:463
  11.6 0.1 conditional.11
  11.6 0.1 branch_1_fun.8
  11.7 11.1 %collective-permute-start.4 = (f32[32,512]{1,0:T(8,128)S(1)}, f32[32,512]{1,0:T(8,128)S(1)}, u32[]{:S(2)}, u32[]{:S(2)}) collective-permute-start(f32[32,512]{1,0:T(8,128)S(1)} %get-tuple-element.140), channel_id=1, source_target_pairs={{0,24},{1,25},{2,26},{3,27},{4,28},{5,29},{6,30},{7,31},{8,16},{9,... | collective-permute-start | bytes 196616 | tf_op jit(solution)/shard_map/ppermute | solution.py:463
  22.8 1.4 %conditional.14 = (f32[80,512]{1,0:T(8,128)S(1)}) conditional(s32[]{:T(128)} %convert_element_type.33, f32[80,512]{1,0:T(8,128)S(1)} %get-tuple-element.157, f32[80,512]{1,0:T(8,128)S(1)} %get-tuple-element.157), branch_computations={%region_8.9_spmd, %region_9.10_spmd} | conditional | bytes 983088 | solution.py:505
  22.8 0.0 collective-permute-start.1
  22.8 1.4 %collective-permute-done.1 = f32[80,512]{1,0:T(8,128)S(1)} collective-permute-done((f32[80,512]{1,0:T(8,128)S(1)}, f32[80,512]{1,0:T(8,128)S(1)}, u32[]{:S(2)}, u32[]{:S(2)}) %collective-permute-start.1) | collective-permute-done | bytes 163872 | tf_op jit(solution)/shard_map/cond/branch_1_fun/ppermute | solution.py:463
  24.2 0.7 %conditional.15 = ((f32[8,32,512]{2,1,0:T(8,128)S(1)}, f32[48,512]{1,0:T(8,128)S(1)})) conditional(s32[]{:T(128)} %convert_element_type.32, (f32[8,32,512]{2,1,0:T(8,128)S(1)}, f32[48,512]{1,0:T(8,128)S(1)}) %tuple.75, (f32[80,512]{1,0:T(8,128)S(1)}, f32[40,512]{1,0:T(8,128)S(1)}, bf16[512,512]{1,0:T(8,128)(2,1)S(1)}) %tuple.76), branch_computations={%region_10.11_spmd, %region_11.12_spmd} | conditional | bytes 8 | solution.py:508
  24.2 0.7 %branch_1_fun.11 = (f32[8,32,512]{2,1,0:T(8,128)S(1)}, f32[48,512]{1,0:T(8,128)S(1)}) custom-call(f32[80,512]{1,0:T(8,128)S(1)} %get-tuple-element.78.between_ref, f32[40,512]{1,0:T(8,128)S(1)} %get-tuple-element.79.above_ref, bf16[512,512]{1,0:T(8,128)(2,1)S(1)} %get-tuple-element.80.pick_ref), custom_call_target="tpu_custom_call" | custom-call | tf_op jit(solution)/shard_map/cond/branch_1_fun/pallas_call | solution.py:510
  25.1 0.5 %collective-permute-done.4 = f32[32,512]{1,0:T(8,128)S(1)} collective-permute-done((f32[32,512]{1,0:T(8,128)S(1)}, f32[32,512]{1,0:T(8,128)S(1)}, u32[]{:S(2)}, u32[]{:S(2)}) %collective-permute-start.4) | collective-permute-done | bytes 65568 | tf_op jit(solution)/shard_map/ppermute | solution.py:463
  25.6 12.3 %conditional.18 = (f32[32,512]{1,0:T(8,128)S(1)}) conditional(s32[]{:T(128)} %convert_element_type.35, f32[32,512]{1,0:T(8,128)S(1)} %get-tuple-element.162, (f32[32,512]{1,0:T(8,128)S(1)}, f32[8,32,512]{2,1,0:T(8,128)S(1)}, f32[48,512]{1,0:T(8,128)S(1)}) %tuple.81), branch_computations={%region_16.17_spmd, %region_17.18_spmd} | conditional | bytes 1048584 | solution.py:536
  25.6 0.7 %branch_1_fun.14 = f32[8,32,512]{2,1,0:T(8,128)S(1)} custom-call(f32[32,512]{1,0:T(8,128)S(1)} %get-tuple-element.86.passed_ref, f32[8,32,512]{2,1,0:T(8,128)S(1)} %get-tuple-element.87.ready_ref, f32[48,512]{1,0:T(8,128)S(1)} %get-tuple-element.88.paths_ref), custom_call_target="tpu_custom_call" | custom-call | tf_op jit(solution)/shard_map/cond/branch_1_fun/pallas_call | solution.py:539
  26.3 11.6 %all_to_all.19.received_ref = f32[8,32,512]{2,1,0:T(8,128)S(1)} all-to-all(f32[8,32,512]{2,1,0:T(8,128)S(1)} %branch_1_fun.14), channel_id=1, replica_groups=mesh['order'=4,'basin'=8] {'basin'}, dimensions={0} | all-to-all | bytes 1048576 | tf_op jit(solution)/shard_map/cond/branch_1_fun/all_to_all | solution.py:395
  37.9 0.7 %shard_map.92 = f32[32,512]{1,0:T(8,128)} custom-call(f32[32,512]{1,0:T(8,128)S(1)} %get-tuple-element.118.runoff_ref, f32[40,512]{1,0:T(8,128)S(1)} %get-tuple-element.119.told_ref, f32[32,512]{1,0:T(8,128)S(1)} %select_add_fusion.arrive_ref), custom_call_target="tpu_custom_call" | custom-call | tf_op jit(solution)/shard_map/pallas_call | solution.py:552
  (11 shorter events, 0.1 us)
Async XLA Ops:
  8.2 3.4 %collective-permute-start = (f32[40,512]{1,0:T(8,128)S(1)}, f32[40,512]{1,0:T(8,128)S(1)}, u32[]{:S(2)}, u32[]{:S(2)}) collective-permute-start(f32[40,512]{1,0:T(8,128)S(1)} %param.1), channel_id=1, source_target_pairs={{0,16},{1,17},{2,18},{3,19},{4,20},{5,21},{6,22},{7,23},{8,24},{9,... | collective-permute-start | bytes 245768 | tf_op jit(solution)/shard_map/cond/branch_1_fun/ppermute | solution.py:463
  11.7 13.8 %collective-permute-start.4 = (f32[32,512]{1,0:T(8,128)S(1)}, f32[32,512]{1,0:T(8,128)S(1)}, u32[]{:S(2)}, u32[]{:S(2)}) collective-permute-start(f32[32,512]{1,0:T(8,128)S(1)} %get-tuple-element.140), channel_id=1, source_target_pairs={{0,24},{1,25},{2,26},{3,27},{4,28},{5,29},{6,30},{7,31},{8,16},{9,... | collective-permute-start | bytes 196616 | tf_op jit(solution)/shard_map/ppermute | solution.py:463
  22.8 1.4 %collective-permute-start.1 = (f32[80,512]{1,0:T(8,128)S(1)}, f32[80,512]{1,0:T(8,128)S(1)}, u32[]{:S(2)}, u32[]{:S(2)}) collective-permute-start(f32[80,512]{1,0:T(8,128)S(1)} %param.9), channel_id=1, source_target_pairs={{0,8},{1,9},{2,10},{3,11},{4,12},{5,13},{6,14},{7,15},{8,0},{9,1},... | collective-permute-start | bytes 491528 | tf_op jit(solution)/shard_map/cond/branch_1_fun/ppermute | solution.py:463
